TPU v7x, 512 devices: a whole 4x4x16 slice. The times are simulated.
512 devices in a mesh: gz: 32 (over y, z_lo), gy: 4 (over z_hi, core), gx: 4 (over x).
Axes of the slice: x: 4, y: 4, z: 16 (z_hi: 2, z_lo: 8; z = z_hi * 8 + z_lo), core: 2. Of those that a mesh axis runs over, the one named last changes fastest.
Arguments:
- images: bfloat16 [32, 320, 2560], P('gz', 'gy', 'gx'), may hold values from -6 to 6
- partner: int32 [4, 4, 32], P('gy', 'gx'), may hold values from 0 to 31, each once within a row
- patch_mask: int32 [32, 4, 32], P('gz', 'gy', 'gx'), may hold values 0 or 1
- flows: bfloat16 [32, 4, 4, 8, 2], P('gz', 'gy', 'gx'), may hold values from -22 to 22
- dest_count: int32 [32, 4, 4, 8], P('gz', 'gy', 'gx'), may hold values from 1 to 2
- dest_owner: int32 [32, 4, 4, 8, 2], P('gz', 'gy', 'gx'), may hold values from 0 to 15, as said below
- dest_cell: int32 [32, 4, 4, 8, 2], P('gz', 'gy', 'gx'), may hold values from 0 to 7
Outputs:
- correlation: float32 [32, 4, 32, 160, 160], P('gz', 'gy', 'gx')
- warped: float32 [32, 320, 2560], P('gz', 'gy', 'gx')
Inputs may be any that keep to these rules, and one draw needn't show every extreme that they name: `partner`: for each tile, a permutation of the 32 sections. `patch_mask`: 1 marks a valid patch. `dest_owner`: owner tiles are numbered tile row times 4 plus tile column, in the block's own section. Counting every entry, live or not, no owner is named more than 2 times by the entries of one tile; in each section one owner is named exactly 2 times by the first entries of every tile of that section. `dest_cell`: cells of the owner tile are numbered row-major over its 1 x 8 cells.
All inputs are finite; a program needn't handle non-finite values. No bound on the sum of `patch_mask` on one device may be relied on, other than what follows from the above.
Results may differ from a plain program's by a relative error of at most 0.0029.
Values may be sent and summed in bfloat16 or wider, within the bound.
A program may use at most 64 MiB of HBM per device.

v0:
```python
import functools

import jax
import jax.numpy as jnp
import ml_dtypes
import numpy as np
from jax import lax
from jax.experimental import pallas as pl
from jax.experimental.pallas import tpu as pltpu
from jax.sharding import PartitionSpec as P

PATCH_SIZE = 160
STRIDE = 80
PATCH_COLS = 8
MARGIN = 24
DEST_SLOTS = 2
BLOCKS = 8
PADDED = 128
SECTIONS = 32
HEIGHT = 80
WIDTH = 640
CHUNKS = 25
LANES = 128
HALO_ROWS = 48
STRIP_ROWS = HEIGHT + 2 * HALO_ROWS
STRIP_COLS = WIDTH + 2 * LANES
HALVES = 9
WAVES = 88
FIXED = 24

epsilon = 1e-05
f32 = jnp.float32
bf16 = jnp.bfloat16
MESH = pl.DeviceIdType.MESH


def halves(table):
    high = table.astype(ml_dtypes.bfloat16)
    low = (table - high.astype(np.float64)).astype(ml_dtypes.bfloat16)
    return high, low


def make_tables():
    wave = np.arange(81)
    place = np.arange(PATCH_SIZE)
    angle = 2.0 * np.pi * (np.outer(wave, place) % PATCH_SIZE) / PATCH_SIZE
    cosine, sine = np.cos(angle), np.sin(angle)
    sine[0] = 0.0
    sine[80] = 0.0
    rows = np.zeros((2 * WAVES, PATCH_SIZE))
    rows[:81] = cosine
    rows[WAVES : WAVES + 81] = sine
    rows_high, rows_low = halves(rows)
    rows_both = np.concatenate([rows_high, rows_low], axis=0)
    row_sums = (rows_high.astype(np.float64) + rows_low.astype(np.float64)).sum(axis=1)
    row_sums = np.broadcast_to(row_sums[:, None], (2 * WAVES, LANES)).astype(np.float32)
    columns = np.zeros((LANES, 2 * LANES))
    columns[:STRIDE, :81] = cosine[:, :STRIDE].T
    columns[:STRIDE, LANES : LANES + 81] = sine[:, :STRIDE].T
    columns_high, columns_low = halves(columns)
    columns_twice = np.concatenate([columns_high, columns_high], axis=0)
    weight = np.ones(81)
    weight[0] = weight[80] = 0.5
    back_columns = np.zeros((2 * LANES, PATCH_SIZE))
    back_columns[:81] = weight[:, None] * cosine
    back_columns[LANES : LANES + 81] = weight[:, None] * sine
    back_columns = halves(back_columns)
    weight = np.full(81, 2.0)
    weight[0] = weight[80] = 1.0
    back_rows = np.zeros((PATCH_SIZE, 2 * WAVES))
    back_rows[:, :81] = (weight[:, None] * cosine).T
    back_rows[:, WAVES : WAVES + 81] = -(weight[:, None] * sine).T
    back_rows = halves(back_rows)
    return (rows_both, row_sums, columns_twice, columns_low, *back_columns, *back_rows)


def table_kernel(owner_ref, cell_ref, count_ref, flow_ref, table_ref, filled_ref):
    for index in range(32):
        table_ref[0, 4 * index] = 0
        table_ref[0, 4 * index + 1] = -1
        table_ref[0, 4 * index + 2] = 0
        table_ref[0, 4 * index + 3] = 0
    for index in range(16):
        filled_ref[index] = 0
    for block in range(BLOCKS):
        count = count_ref[block]
        for entry in range(DEST_SLOTS):

            @pl.when(entry < count)
            def _():
                owner = owner_ref[2 * block + entry]
                rank = filled_ref[owner]
                filled_ref[owner] = rank + 1
                base = 8 * owner + 4 * rank
                table_ref[0, base] = block
                table_ref[0, base + 1] = cell_ref[2 * block + entry]
                table_ref[0, base + 2] = flow_ref[2 * block]
                table_ref[0, base + 3] = flow_ref[2 * block + 1]


def chunk_of(index):
    line, place = index // 8, index % 8
    holds = ((place >= 1) & (place <= 6)) | (index == 0)
    return holds, jnp.where(index == 0, CHUNKS - 1, line * 6 + place - 1)


def holder_of(chunk):
    return jnp.where(chunk == CHUNKS - 1, 0, (chunk // 6) * 8 + chunk % 6 + 1)


def chunk_at(ref, chunk, row, column):
    rows = pl.ds(pl.multiple_of(row + 16 * (chunk // 5), 16), 16)
    columns = pl.ds(pl.multiple_of(column + LANES * (chunk % 5), LANES), LANES)
    return ref.at[rows, columns]


def exchange_kernel(
    tile_ref,
    partner_ref,
    table_ref,
    table_smem,
    own_ref,
    other_ref,
    slots_ref,
    info_ref,
    held,
    sorted_,
    mirror,
    blocks,
    outgoing,
    tables,
    mirror_smem,
    send_sem,
    recv_sem,
    far_sem,
    slot_sem,
    local_sem,
):
    gz, gy, gx = lax.axis_index("gz"), lax.axis_index("gy"), lax.axis_index("gx")
    half, core = gy // 2, gy % 2
    place = core * 4 + gx
    far_gy = 3 - gy
    near_gy = gy + 1 - 2 * core

    barrier = pltpu.get_barrier_semaphore()

    def greet(step, carry):
        pl.semaphore_signal(
            barrier, inc=1, device_id={"gz": lax.rem(gz + step, SECTIONS)}, device_id_type=MESH
        )
        return carry

    lax.fori_loop(1, SECTIONS, greet, 0)
    for step in range(1, 8):
        other_place = lax.rem(place + step, 8)
        pl.semaphore_signal(
            barrier,
            inc=1,
            device_id={"gy": 2 * half + other_place // 4, "gx": other_place % 4},
            device_id_type=MESH,
        )
    pl.semaphore_signal(barrier, inc=1, device_id={"gy": far_gy}, device_id_type=MESH)

    tables[0] = table_ref[...]
    own_ref[pl.ds(HALO_ROWS, HEIGHT), pl.ds(LANES, WIDTH)] = tile_ref[...]
    top, bottom = pl.ds(0, HALO_ROWS), pl.ds(HALO_ROWS + HEIGHT, HALO_ROWS)
    left, right = pl.ds(0, LANES), pl.ds(LANES + WIDTH, LANES)
    middle = pl.ds(LANES, WIDTH)
    for ref in (own_ref, other_ref):

        @pl.when(gy == 0)
        def _():
            ref[top, middle] = jnp.zeros((HALO_ROWS, WIDTH), bf16)

        @pl.when(gy == 3)
        def _():
            ref[bottom, middle] = jnp.zeros((HALO_ROWS, WIDTH), bf16)

        @pl.when(gx == 0)
        def _():
            ref[:, left] = jnp.zeros((STRIP_ROWS, LANES), bf16)

        @pl.when(gx == 3)
        def _():
            ref[:, right] = jnp.zeros((STRIP_ROWS, LANES), bf16)

    holds, mine = chunk_of(gz)
    pl.semaphore_wait(barrier, SECTIONS - 1 + 8)

    def scatter(step, carry):
        chunk = lax.rem(mine + step, CHUNKS)
        holder = holder_of(chunk)

        @pl.when(holder != gz)
        def _():
            pltpu.make_async_remote_copy(
                src_ref=chunk_at(tile_ref, chunk, 0, 0),
                dst_ref=held.at[gz],
                send_sem=send_sem.at[0],
                recv_sem=recv_sem.at[0],
                device_id={"gz": holder},
                device_id_type=MESH,
            ).start()

        return carry

    lax.fori_loop(0, CHUNKS, scatter, 0)

    def copy(src, dst, slot, device):
        return pltpu.make_async_remote_copy(
            src_ref=src,
            dst_ref=dst,
            send_sem=far_sem.at[0, slot],
            recv_sem=far_sem.at[1, slot],
            device_id=device,
            device_id_type=MESH,
        )

    near = {"gy": near_gy}

    own_down = copy(
        tile_ref.at[pl.ds(HEIGHT - HALO_ROWS, HALO_ROWS), :], own_ref.at[top, middle], 0, near
    )
    own_up = copy(tile_ref.at[pl.ds(0, HALO_ROWS), :], own_ref.at[bottom, middle], 0, near)

    @pl.when(core == 0)
    def _():
        own_down.start()

    @pl.when(core == 1)
    def _():
        own_up.start()

    to_far = copy(tile_ref, mirror, 1, {"gy": far_gy})
    to_far.start()
    table_far = copy(tables.at[0], tables.at[1], 2, {"gy": far_gy})
    table_far.start()

    lane = lax.broadcasted_iota(jnp.int32, (HEIGHT, LANES), 1)

    def cut_blocks(ref, base):
        for block in range(BLOCKS):
            start = STRIDE * block
            first = start // LANES * LANES
            shift = start - first
            width = LANES if shift + STRIDE <= LANES else 2 * LANES
            window = ref[:, first : first + width].astype(f32)
            if shift:
                window = pltpu.roll(window, width - shift, 1)[:, :LANES]
            blocks[base + block] = jnp.where(lane < STRIDE, window, 0.0).astype(bf16)

    cut_blocks(tile_ref, 0)

    @pl.when(holds)
    def _():
        held[gz] = chunk_at(tile_ref, mine, 0, 0)[...]
        pltpu.make_async_copy(
            held.at[pl.ds(0, SECTIONS - 1)], held.at[pl.ds(0, SECTIONS - 1)], recv_sem.at[0]
        ).wait()

        def deliver(step, carry):
            section = lax.rem(gz + step, SECTIONS)
            sorted_[section] = held[partner_ref[section]]
            pltpu.make_async_remote_copy(
                src_ref=sorted_.at[section],
                dst_ref=chunk_at(other_ref, mine, HALO_ROWS, LANES),
                send_sem=send_sem.at[1],
                recv_sem=recv_sem.at[1],
                device_id={"gz": section},
                device_id_type=MESH,
            ).start()
            return carry

        lax.fori_loop(1, SECTIONS, deliver, 0)
        chunk_at(other_ref, mine, HALO_ROWS, LANES)[...] = held[partner_ref[gz]]

    def side_copies(ref, slot):
        to_right = copy(
            ref.at[:, pl.ds(WIDTH, LANES)], ref.at[:, left], slot, {"gx": jnp.minimum(gx + 1, 3)}
        )
        to_left = copy(
            ref.at[:, pl.ds(LANES, LANES)], ref.at[:, right], slot + 1, {"gx": jnp.maximum(gx - 1, 0)}
        )
        return to_right, to_left

    def start_sides(copies):
        @pl.when(gx < 3)
        def _():
            copies[0].start()

        @pl.when(gx > 0)
        def _():
            copies[1].start()

    def receive_sides(copies):
        @pl.when(gx > 0)
        def _():
            copies[0].wait_recv()

        @pl.when(gx < 3)
        def _():
            copies[1].wait_recv()

    def sent_sides(copies):
        @pl.when(gx < 3)
        def _():
            copies[0].wait_send()

        @pl.when(gx > 0)
        def _():
            copies[1].wait_send()

    @pl.when(core == 1)
    def _():
        own_down.wait_recv()

    @pl.when(core == 0)
    def _():
        own_up.wait_recv()

    to_far.wait_recv()

    @pl.when(gy == 1)
    def _():
        own_ref[bottom, middle] = mirror[pl.ds(0, HALO_ROWS), :]

    @pl.when(gy == 2)
    def _():
        own_ref[top, middle] = mirror[pl.ds(HEIGHT - HALO_ROWS, HALO_ROWS), :]

    own_sides = side_copies(own_ref, 3)
    start_sides(own_sides)

    table_far.wait_recv()
    fetch = pltpu.make_async_copy(tables.at[1], mirror_smem, local_sem)
    fetch.start()
    cut_blocks(mirror, BLOCKS)
    fetch.wait()

    def fill(target, index):
        owner = 8 * half + target
        for kind, table in ((0, table_smem), (1, mirror_smem)):
            for rank in range(2):
                block = table[0, 8 * owner + 4 * rank]
                index[2 * kind + rank] = blocks[BLOCKS * kind + block]

    def send_slots(step, carry):
        target = lax.rem(place + step, 8)
        fill(target, outgoing.at[target])
        device = {"gy": 2 * half + target // 4, "gx": target % 4}
        for src, dst, kind in (
            (outgoing.at[target], slots_ref.at[place], 0),
            (tables, info_ref.at[place], 1),
        ):
            pltpu.make_async_remote_copy(
                src_ref=src,
                dst_ref=dst,
                send_sem=slot_sem.at[0, kind],
                recv_sem=slot_sem.at[1, kind],
                device_id=device,
                device_id_type=MESH,
            ).start()
        return carry

    lax.fori_loop(1, 8, send_slots, 0)
    fill(place, slots_ref.at[place])
    info_ref[place] = tables[...]

    chunks = held.at[pl.ds(0, CHUNKS)]
    fewer = held.at[pl.ds(0, CHUNKS - 1)]

    @pl.when(holds)
    def _():
        pltpu.make_async_copy(fewer, fewer, recv_sem.at[1]).wait()

    @pl.when(jnp.logical_not(holds))
    def _():
        pltpu.make_async_copy(chunks, chunks, recv_sem.at[1]).wait()

    rows_up = pl.ds(HALO_ROWS, HALO_ROWS)
    rows_down = pl.ds(HEIGHT, HALO_ROWS)
    other_down = copy(
        other_ref.at[rows_down, middle], other_ref.at[top, middle], 5, {"gy": jnp.minimum(gy + 1, 3)}
    )
    other_up = copy(
        other_ref.at[rows_up, middle], other_ref.at[bottom, middle], 6, {"gy": jnp.maximum(gy - 1, 0)}
    )

    @pl.when(gy < 3)
    def _():
        other_down.start()

    @pl.when(gy > 0)
    def _():
        other_up.start()

    @pl.when(gy > 0)
    def _():
        other_down.wait_recv()

    @pl.when(gy < 3)
    def _():
        other_up.wait_recv()

    other_sides = side_copies(other_ref, 7)
    start_sides(other_sides)

    receive_sides(own_sides)
    seven = slots_ref.at[pl.ds(0, 7)]
    pltpu.make_async_copy(seven, seven, slot_sem.at[1, 0]).wait()
    seven_info = info_ref.at[pl.ds(0, 7)]
    pltpu.make_async_copy(seven_info, seven_info, slot_sem.at[1, 1]).wait()
    receive_sides(other_sides)

    pltpu.make_async_copy(seven, seven, slot_sem.at[0, 0]).wait()
    pltpu.make_async_copy(seven_info, seven_info, slot_sem.at[0, 1]).wait()

    @pl.when(holds)
    def _():
        pltpu.make_async_copy(fewer, fewer, send_sem.at[0]).wait()
        all_but_one = held.at[pl.ds(0, SECTIONS - 1)]
        pltpu.make_async_copy(all_but_one, all_but_one, send_sem.at[1]).wait()

    @pl.when(jnp.logical_not(holds))
    def _():
        pltpu.make_async_copy(chunks, chunks, send_sem.at[0]).wait()

    @pl.when(core == 0)
    def _():
        own_down.wait_send()

    @pl.when(core == 1)
    def _():
        own_up.wait_send()

    to_far.wait_send()
    table_far.wait_send()

    @pl.when(gy < 3)
    def _():
        other_down.wait_send()

    @pl.when(gy > 0)
    def _():
        other_up.wait_send()

    sent_sides(own_sides)
    sent_sides(other_sides)


def split(value):
    high = value.astype(bf16)
    return high, (value - high.astype(f32)).astype(bf16)


def dot(left, right):
    return jnp.dot(left, right, preferred_element_type=f32)


def compute_kernel(
    own_ref,
    other_ref,
    slots_ref,
    info_ref,
    mask_ref,
    place_ref,
    rows_both,
    row_sums,
    columns_twice,
    columns_low,
    back_columns_high,
    back_columns_low,
    back_rows_high,
    back_rows_low,
    correlation_ref,
    warped_ref,
    strip,
    spectra,
    parts,
    cells,
    shifted,
    canvas,
):
    lane = lax.broadcasted_iota(jnp.int32, (PATCH_SIZE, LANES), 1)
    means, squares = [], []
    for index, ref in enumerate((own_ref, other_ref)):
        for block in range(HALVES):
            start = LANES - 40 + STRIDE * block
            first = start // LANES * LANES
            shift = start - first
            width = LANES if shift + STRIDE <= LANES else 2 * LANES
            window = ref[8 : 8 + PATCH_SIZE, first : first + width].astype(f32)
            window = pltpu.roll(window, width - shift, 1)[:, :LANES]
            window = jnp.where(lane < STRIDE, window, 0.0)
            mean = jnp.sum(window, keepdims=True) * (1.0 / (PATCH_SIZE * STRIDE))
            centred = jnp.where(lane < STRIDE, window - mean, 0.0)
            means.append(mean)
            squares.append(jnp.sum(centred * centred, keepdims=True))
            strip[:, pl.ds((index * HALVES + block) * LANES, LANES)] = window.astype(bf16)

    levels = [sum(means[:HALVES]) * (1.0 / HALVES), sum(means[HALVES:]) * (1.0 / HALVES)]
    for block in range(2 * HALVES):
        both = dot(rows_both[...], strip[:, pl.ds(block * LANES, LANES)])
        value = both[: 2 * WAVES] + both[2 * WAVES :] - levels[block // HALVES] * row_sums[...]
        high, low = split(value)
        spectra[block, :, :LANES] = high
        spectra[block, :, LANES:] = low
    for block in range(2 * HALVES):
        parts[block] = dot(spectra[block], columns_twice[...]) + dot(
            spectra[block, :, :LANES], columns_low[...]
        )

    row = lax.broadcasted_iota(jnp.int32, (WAVES, LANES), 0)
    column = lax.broadcasted_iota(jnp.int32, (WAVES, LANES), 1)
    constant = (row == 0) & (column == 0)
    odd = column % 2 == 1
    count = PATCH_SIZE * STRIDE

    def spectrum(first):
        def one(rows, lanes):
            later = parts[first + 1, rows, lanes]
            return parts[first, rows, lanes] + jnp.where(odd, -later, later)

        upper, lower = pl.ds(0, WAVES), pl.ds(WAVES, WAVES)
        low, high = pl.ds(0, LANES), pl.ds(LANES, LANES)
        a = jnp.where(constant, 0.0, one(upper, low))
        return a, one(lower, high), one(lower, low), one(upper, high)

    for patch in range(PATCH_COLS):
        scale = mask_ref[0, patch].astype(f32) * (1.0 / PATCH_SIZE**3)
        for base in (0, HALVES):
            first, second = base + patch, base + patch + 1
            gap = means[first] - means[second]
            spread = (squares[first] + squares[second] + gap * gap * (count / 2)) * (0.5 / count)
            scale = scale / jnp.sqrt(spread + epsilon)
        a, b, c, d = spectrum(patch)
        e, f, g, h = spectrum(HALVES + patch)
        scale = 2.0 * scale
        even_real = (a * e + b * f + c * g + d * h) * scale
        odd_real = (c * h + d * g - a * f - b * e) * scale
        even_imag = (c * e - d * f - a * g + b * h) * scale
        odd_imag = (d * e - c * f - a * h + b * g) * scale
        joined = jnp.concatenate(
            [
                jnp.concatenate([even_real, -odd_imag], axis=1),
                jnp.concatenate([even_imag, odd_real], axis=1),
            ],
            axis=0,
        )
        high, low = split(joined)
        half = (
            dot(high, back_columns_high[...])
            + dot(low, back_columns_high[...])
            + dot(high, back_columns_low[...])
        )
        high, low = split(half)
        correlation_ref[patch] = (
            dot(back_rows_high[...], high)
            + dot(back_rows_high[...], low)
            + dot(back_rows_low[...], high)
        )

    cells[...] = jnp.zeros_like(cells)
    shifted[...] = jnp.zeros_like(shifted)
    mine = place_ref[0] * 8

    def entry(index, carry):
        source, kind, rank = index // 4, index % 4 // 2, index % 2
        base = mine + 4 * rank
        cell = info_ref[source, kind, 0, base + 1]

        @pl.when(cell >= 0)
        def _():
            down, across = info_ref[source, kind, 0, base + 2], info_ref[source, kind, 0, base + 3]
            whole_down, whole_across = down >> FIXED, across >> FIXED
            unit = 1.0 / 2**FIXED
            part_down = (down & (2**FIXED - 1)).astype(f32) * unit
            part_across = (across & (2**FIXED - 1)).astype(f32) * unit
            block = slots_ref[source, 2 * kind + rank].astype(f32)
            here = pltpu.roll(block, whole_across + MARGIN, 1)
            after = pltpu.roll(block, whole_across + MARGIN + 1, 1)
            shifted[pl.ds(MARGIN, HEIGHT), :] = here * (1.0 - part_across) + after * part_across
            here = shifted[pl.ds(MARGIN - whole_down, HEIGHT), :]
            after = shifted[pl.ds(MARGIN - 1 - whole_down, HEIGHT), :]
            value = here * (1.0 - part_down) + after * part_down
            cells[cell] = cells[cell] + value.astype(bf16).astype(f32)

        return carry

    lax.fori_loop(0, 32, entry, 0)
    canvas[...] = jnp.zeros_like(canvas)
    for cell in range(BLOCKS):
        start = LANES - MARGIN + STRIDE * cell
        first = start // LANES * LANES
        shift = start - first
        wide = jnp.concatenate([cells[cell], jnp.zeros((HEIGHT, LANES), f32)], axis=1)
        if shift:
            wide = pltpu.roll(wide, shift, 1)
        canvas[:, first : first + 2 * LANES] = canvas[:, first : first + 2 * LANES] + wide
    warped_ref[...] = canvas[:, LANES : LANES + WIDTH]


VMEM = pl.BlockSpec(memory_space=pltpu.VMEM)
SMEM = pl.BlockSpec(memory_space=pltpu.SMEM)


def body(tables, images, partner, patch_mask, flows, dest_count, dest_owner, dest_cell):
    tile = images[0]
    fixed = jnp.round(flows.astype(f32) * float(2**FIXED)).astype(jnp.int32).reshape(16)
    table = pl.pallas_call(
        table_kernel,
        out_shape=jax.ShapeDtypeStruct((1, 128), jnp.int32),
        in_specs=[SMEM] * 4,
        out_specs=SMEM,
        scratch_shapes=[pltpu.SMEM((16,), jnp.int32)],
    )(dest_owner.reshape(16), dest_cell.reshape(16), dest_count.reshape(8), fixed)
    own, other, slots, info = pl.pallas_call(
        exchange_kernel,
        out_shape=[
            jax.ShapeDtypeStruct((STRIP_ROWS, STRIP_COLS), bf16),
            jax.ShapeDtypeStruct((STRIP_ROWS, STRIP_COLS), bf16),
            jax.ShapeDtypeStruct((8, 4, HEIGHT, LANES), bf16),
            jax.ShapeDtypeStruct((8, 2, 1, 128), jnp.int32),
        ],
        in_specs=[VMEM, SMEM, VMEM, SMEM],
        out_specs=[VMEM] * 4,
        scratch_shapes=[
            pltpu.VMEM((SECTIONS, 16, LANES), bf16),
            pltpu.VMEM((SECTIONS, 16, LANES), bf16),
            pltpu.VMEM((HEIGHT, WIDTH), bf16),
            pltpu.VMEM((2 * BLOCKS, HEIGHT, LANES), bf16),
            pltpu.VMEM((8, 4, HEIGHT, LANES), bf16),
            pltpu.VMEM((2, 1, 128), jnp.int32),
            pltpu.SMEM((1, 128), jnp.int32),
            pltpu.SemaphoreType.DMA((2,)),
            pltpu.SemaphoreType.DMA((2,)),
            pltpu.SemaphoreType.DMA((2, 9)),
            pltpu.SemaphoreType.DMA((2, 2)),
            pltpu.SemaphoreType.DMA,
        ],
        compiler_params=pltpu.CompilerParams(
            collective_id=0, has_side_effects=True, vmem_limit_bytes=24 * 2**20
        ),
    )(tile, partner.reshape(SECTIONS), table, table)
    place = (lax.axis_index("gy") * 4 + lax.axis_index("gx")).astype(jnp.int32).reshape(1)
    correlation, warped = pl.pallas_call(
        compute_kernel,
        out_shape=[
            jax.ShapeDtypeStruct((PATCH_COLS, PATCH_SIZE, PATCH_SIZE), f32),
            jax.ShapeDtypeStruct((HEIGHT, WIDTH), f32),
        ],
        in_specs=[VMEM, VMEM, VMEM, SMEM, SMEM, SMEM] + [VMEM] * 8,
        out_specs=[VMEM] * 2,
        scratch_shapes=[
            pltpu.VMEM((PATCH_SIZE, 2 * HALVES * LANES), bf16),
            pltpu.VMEM((2 * HALVES, 2 * WAVES, 2 * LANES), bf16),
            pltpu.VMEM((2 * HALVES, 2 * WAVES, 2 * LANES), f32),
            pltpu.VMEM((BLOCKS, HEIGHT, LANES), f32),
            pltpu.VMEM((128, LANES), f32),
            pltpu.VMEM((HEIGHT, STRIP_COLS), f32),
        ],
        compiler_params=pltpu.CompilerParams(vmem_limit_bytes=40 * 2**20),
    )(own, other, slots, info, patch_mask[0], place, *tables)
    return correlation[None, None], warped[None]


def solution(mesh):
    placed = (
        P("gz", "gy", "gx"),
        P("gy", "gx", None),
        P("gz", "gy", "gx"),
        P("gz", "gy", "gx", None, None),
        P("gz", "gy", "gx", None),
        P("gz", "gy", "gx", None, None),
        P("gz", "gy", "gx", None, None),
    )
    tables = tuple(jnp.asarray(table) for table in make_tables())
    return jax.shard_map(
        functools.partial(body, tables),
        mesh=mesh,
        in_specs=placed,
        out_specs=(P("gz", "gy", "gx", None, None), P("gz", "gy", "gx")),
        check_vma=False,
    )
```

profile of v0, /device:TPU:1, one launch (start us, length us, event | category | flops | bytes accessed | tf_op | source)
XLA Modules:
  0.0 80.1 jit_solution(4359038497148742830)
XLA Ops:
  0.6 0.7 round-nearest-even_convert_fusion
  1.3 0.1 copy.22
  1.4 0.6 reshape.26.flow_ref
  2.0 0.8 copy.20
  2.8 0.6 reshape.23.owner_ref
  3.4 0.8 copy.21
  4.1 0.6 reshape.24.cell_ref
  4.7 1.4 %shard_map.158.table_ref.table_smem = s32[1,128]{1,0:T(1,128)} custom-call(s32[16]{0:T(128)} %reshape.23.owner_ref, s32[16]{0:T(128)} %reshape.24.cell_ref, s32[8]{0:T(128)} %bitcast.16, s32[16]{0:T(128)} %reshape.26.flow_ref), custom_call_target="tpu_custom_call" | custom-call | tf_op jit(solution)/shard_map/pallas_call | solution.py:610
  6.1 0.0 copy-start.4
  6.1 0.9 %copy-done.4 = bf16[1,80,640]{2,1,0:T(8,128)(2,1)S(1)} copy-done((bf16[1,80,640]{2,1,0:T(8,128)(2,1)S(1)}, bf16[1,80,640]{2,1,0:T(8,128)(2,1)}, u32[]{:S(2)}) %copy-start.4) | copy-done | bytes 102424
  7.0 0.0 copy-start.9
  7.0 0.7 copy-done.9
  7.7 0.0 copy-start.10
  7.7 0.7 copy-done.10
  8.3 52.6 %shard_map.159 = (bf16[176,896]{1,0:T(8,128)(2,1)S(1)}, bf16[176,896]{1,0:T(8,128)(2,1)S(1)}, bf16[8,4,80,128]{3,2,1,0:T(8,128)(2,1)S(1)}, s32[8,2,1,128]{3,2,1,0:T(1,128)S(1)}) custom-call(bf16[80,640]{1,0:T(8,128)(2,1)S(1)} %bitcast.13, s32[32]{0:T(128)S(1)} %bitcast.14, s32[1,128]{1,0:T(1,128)S(1)} %copy-done.9, s32[1,128]{1,0:T(1,128)S(1)} %copy-done.9), custom_call_target="tpu_custom_call" | custom-call | tf_op jit(solution)/shard_map/pallas_call | solution.py:617
  61.0 0.0 copy-start
  61.0 0.9 %copy-done = bf16[352,160]{1,0:T(8,128)(2,1)S(1)} copy-done((bf16[352,160]{1,0:T(8,128)(2,1)S(1)}, bf16[352,160]{1,0:T(8,128)(2,1)}, u32[]{:S(2)}) %copy-start) | copy-done | bytes 112664
  61.9 0.0 copy-start.1
  61.9 0.9 %copy-done.1 = bf16[256,160]{1,0:T(8,128)(2,1)S(1)} copy-done((bf16[256,160]{1,0:T(8,128)(2,1)S(1)}, bf16[256,160]{1,0:T(8,128)(2,1)}, u32[]{:S(2)}) %copy-start.1) | copy-done | bytes 81944
  62.8 0.0 copy-start.2
  62.8 0.9 %copy-done.2 = bf16[256,160]{1,0:T(8,128)(2,1)S(1)} copy-done((bf16[256,160]{1,0:T(8,128)(2,1)S(1)}, bf16[256,160]{1,0:T(8,128)(2,1)}, u32[]{:S(2)}) %copy-start.2) | copy-done | bytes 81944
  63.7 0.0 copy-start.3
  63.7 0.9 %copy-done.3 = bf16[256,256]{1,0:T(8,128)(2,1)S(1)} copy-done((bf16[256,256]{1,0:T(8,128)(2,1)S(1)}, bf16[256,256]{1,0:T(8,128)(2,1)}, u32[]{:S(2)}) %copy-start.3) | copy-done | bytes 131096
  64.6 0.0 copy-start.5
  64.6 0.9 %copy-done.5 = f32[176,128]{1,0:T(8,128)S(1)} copy-done((f32[176,128]{1,0:T(8,128)S(1)}, f32[176,128]{1,0:T(8,128)}, u32[]{:S(2)}) %copy-start.5) | copy-done | bytes 90136
  65.5 0.0 copy-start.6
  65.5 0.9 %copy-done.6 = bf16[160,176]{1,0:T(8,128)(2,1)S(1)} copy-done((bf16[160,176]{1,0:T(8,128)(2,1)S(1)}, bf16[160,176]{1,0:T(8,128)(2,1)}, u32[]{:S(2)}) %copy-start.6) | copy-done | bytes 56344
  66.4 0.0 copy-start.7
  66.4 0.9 %copy-done.7 = bf16[160,176]{1,0:T(8,128)(2,1)S(1)} copy-done((bf16[160,176]{1,0:T(8,128)(2,1)S(1)}, bf16[160,176]{1,0:T(8,128)(2,1)}, u32[]{:S(2)}) %copy-start.7) | copy-done | bytes 56344
  67.3 0.0 copy-start.8
  67.3 0.8 %copy-done.8 = bf16[128,256]{1,0:T(8,128)(2,1)S(1)} copy-done((bf16[128,256]{1,0:T(8,128)(2,1)S(1)}, bf16[128,256]{1,0:T(8,128)(2,1)}, u32[]{:S(2)}) %copy-start.8) | copy-done | bytes 65560
  68.1 0.0 copy-start.11
  68.1 0.7 copy-done.11
  68.8 11.3 %shard_map.160 = (f32[8,160,160]{2,1,0:T(8,128)}, f32[80,640]{1,0:T(8,128)}) custom-call(bf16[176,896]{1,0:T(8,128)(2,1)S(1)} %get-tuple-element.8.own_ref, bf16[176,896]{1,0:T(8,128)(2,1)S(1)} %get-tuple-element.9.other_ref, bf16[8,4,80,128]{3,2,1,0:T(8,128)(2,1)S(1)} %get-tuple-element.10.slots_ref, s32[8,2,1,128]{3,2,1,0:T(1,128)S(1)} %get-tuple-element.11.info_ref, ...), custom_call_target="tpu_custom_call" | custom-call | tf_op jit(solution)/shard_map/pallas_call | solution.py:646
Async XLA Ops:
  6.1 0.9 %copy-start.4 = (bf16[1,80,640]{2,1,0:T(8,128)(2,1)S(1)}, bf16[1,80,640]{2,1,0:T(8,128)(2,1)}, u32[]{:S(2)}) copy-start(bf16[1,80,640]{2,1,0:T(8,128)(2,1)} %param.15) | copy-start | bytes 307204
  7.0 0.7 copy-start.9
  7.7 0.7 copy-start.10
  61.0 0.9 %copy-start = (bf16[352,160]{1,0:T(8,128)(2,1)S(1)}, bf16[352,160]{1,0:T(8,128)(2,1)}, u32[]{:S(2)}) copy-start(bf16[352,160]{1,0:T(8,128)(2,1)} %constant.27.clone.rows_both) | copy-start | bytes 337924
  61.9 0.9 %copy-start.1 = (bf16[256,160]{1,0:T(8,128)(2,1)S(1)}, bf16[256,160]{1,0:T(8,128)(2,1)}, u32[]{:S(2)}) copy-start(bf16[256,160]{1,0:T(8,128)(2,1)} %constant.32.clone.back_columns_low) | copy-start | bytes 245764
  62.8 0.9 %copy-start.2 = (bf16[256,160]{1,0:T(8,128)(2,1)S(1)}, bf16[256,160]{1,0:T(8,128)(2,1)}, u32[]{:S(2)}) copy-start(bf16[256,160]{1,0:T(8,128)(2,1)} %constant.31.clone.back_columns_high) | copy-start | bytes 245764
  63.7 0.9 %copy-start.3 = (bf16[256,256]{1,0:T(8,128)(2,1)S(1)}, bf16[256,256]{1,0:T(8,128)(2,1)}, u32[]{:S(2)}) copy-start(bf16[256,256]{1,0:T(8,128)(2,1)} %constant.29.clone.columns_twice) | copy-start | bytes 393220
  64.6 0.9 %copy-start.5 = (f32[176,128]{1,0:T(8,128)S(1)}, f32[176,128]{1,0:T(8,128)}, u32[]{:S(2)}) copy-start(f32[176,128]{1,0:T(8,128)} %constant.28.clone.row_sums) | copy-start | bytes 270340
  65.5 0.9 %copy-start.6 = (bf16[160,176]{1,0:T(8,128)(2,1)S(1)}, bf16[160,176]{1,0:T(8,128)(2,1)}, u32[]{:S(2)}) copy-start(bf16[160,176]{1,0:T(8,128)(2,1)} %constant.34.clone.back_rows_low) | copy-start | bytes 168964
  66.4 0.9 %copy-start.7 = (bf16[160,176]{1,0:T(8,128)(2,1)S(1)}, bf16[160,176]{1,0:T(8,128)(2,1)}, u32[]{:S(2)}) copy-start(bf16[160,176]{1,0:T(8,128)(2,1)} %constant.33.clone.back_rows_high) | copy-start | bytes 168964
  67.3 0.8 %copy-start.8 = (bf16[128,256]{1,0:T(8,128)(2,1)S(1)}, bf16[128,256]{1,0:T(8,128)(2,1)}, u32[]{:S(2)}) copy-start(bf16[128,256]{1,0:T(8,128)(2,1)} %constant.30.clone.columns_low) | copy-start | bytes 196612
  68.1 0.7 copy-start.11
where the time goes:
time: 80.5 us; the launch traced here: 80.1 us
  Pallas kernels  65.3 us (81%)
  local copies, waits for them, and re-layouts  13.4 us (17%)
    pallas_call x1, Pallas kernels, body(): pl.pallas_call(exchange_kernel, out_shape=[jax.ShapeDtypeStruct((STRIP_RO...  52.6 us
    unnamed x26, local copies, waits for them, and re-layouts  11.5 us
    pallas_call x1, Pallas kernels, body(): pl.pallas_call(compute_kernel, out_shape=[jax.ShapeDtypeStruct((PATCH_COL...  11.3 us

commit v1 on v0

--- a/solution.py
+++ b/solution.py
@@ -15,6 +15,7 @@
 MARGIN = 24
 DEST_SLOTS = 2
 BLOCKS = 8
+OWNERS = 16
 PADDED = 128
 SECTIONS = 32
 HEIGHT = 80
@@ -26,6 +27,7 @@
 STRIP_COLS = WIDTH + 2 * LANES
 HALVES = 9
 WAVES = 88
+VMEM_BYTES = 60 * 2**20
 FIXED = 24
 
 epsilon = 1e-05
@@ -74,28 +76,30 @@
     return (rows_both, row_sums, columns_twice, columns_low, *back_columns, *back_rows)
 
 
-def table_kernel(owner_ref, cell_ref, count_ref, flow_ref, table_ref, filled_ref):
-    for index in range(32):
-        table_ref[0, 4 * index] = 0
-        table_ref[0, 4 * index + 1] = -1
-        table_ref[0, 4 * index + 2] = 0
-        table_ref[0, 4 * index + 3] = 0
-    for index in range(16):
-        filled_ref[index] = 0
+def fill_table(owner_ref, cell_ref, count_ref, flow_ref, table_ref):
+    owners, codes = [], []
     for block in range(BLOCKS):
-        count = count_ref[block]
         for entry in range(DEST_SLOTS):
-
-            @pl.when(entry < count)
-            def _():
-                owner = owner_ref[2 * block + entry]
-                rank = filled_ref[owner]
-                filled_ref[owner] = rank + 1
-                base = 8 * owner + 4 * rank
-                table_ref[0, base] = block
-                table_ref[0, base + 1] = cell_ref[2 * block + entry]
-                table_ref[0, base + 2] = flow_ref[2 * block]
-                table_ref[0, base + 3] = flow_ref[2 * block + 1]
+            live = entry < count_ref[0, block]
+            owners.append(jnp.where(live, owner_ref[entry, block], -1))
+            codes.append(BLOCKS * block + cell_ref[entry, block])
+
+    def one(owner, carry):
+        first = second = jnp.int32(-1)
+        for named, code in zip(owners, codes):
+            match = named == owner
+            second = jnp.where(match, first, second)
+            first = jnp.where(match, code, first)
+        for rank, code in enumerate((first, second)):
+            block = jnp.maximum(code, 0) >> 3
+            base = 8 * owner + 4 * rank
+            table_ref[0, base] = block
+            table_ref[0, base + 1] = jnp.where(code < 0, -1, code & 7)
+            table_ref[0, base + 2] = flow_ref[0, block]
+            table_ref[0, base + 3] = flow_ref[1, block]
+        return carry
+
+    lax.fori_loop(0, OWNERS, one, 0)
 
 
 def chunk_of(index):
@@ -117,8 +121,10 @@
 def exchange_kernel(
     tile_ref,
     partner_ref,
-    table_ref,
-    table_smem,
+    owner_ref,
+    cell_ref,
+    count_ref,
+    flow_ref,
     own_ref,
     other_ref,
     slots_ref,
@@ -129,6 +135,9 @@
     blocks,
     outgoing,
     tables,
+    fixed,
+    fixed_smem,
+    table_smem,
     mirror_smem,
     send_sem,
     recv_sem,
@@ -161,7 +170,9 @@
         )
     pl.semaphore_signal(barrier, inc=1, device_id={"gy": far_gy}, device_id_type=MESH)
 
-    tables[0] = table_ref[...]
+    fixed[...] = jnp.round(flow_ref[...].astype(f32) * float(2**FIXED)).astype(jnp.int32)
+    to_scalars = pltpu.make_async_copy(fixed, fixed_smem, local_sem)
+    to_scalars.start()
     own_ref[pl.ds(HALO_ROWS, HEIGHT), pl.ds(LANES, WIDTH)] = tile_ref[...]
     top, bottom = pl.ds(0, HALO_ROWS), pl.ds(HALO_ROWS + HEIGHT, HALO_ROWS)
     left, right = pl.ds(0, LANES), pl.ds(LANES + WIDTH, LANES)
@@ -233,6 +244,11 @@
 
     to_far = copy(tile_ref, mirror, 1, {"gy": far_gy})
     to_far.start()
+    to_scalars.wait()
+    fill_table(owner_ref, cell_ref, count_ref, fixed_smem, table_smem)
+    to_vector = pltpu.make_async_copy(table_smem, tables.at[0], local_sem)
+    to_vector.start()
+    to_vector.wait()
     table_far = copy(tables.at[0], tables.at[1], 2, {"gy": far_gy})
     table_far.start()
 
@@ -260,7 +276,7 @@
 
         def deliver(step, carry):
             section = lax.rem(gz + step, SECTIONS)
-            sorted_[section] = held[partner_ref[section]]
+            sorted_[section] = held[partner_ref[0, section]]
             pltpu.make_async_remote_copy(
                 src_ref=sorted_.at[section],
                 dst_ref=chunk_at(other_ref, mine, HALO_ROWS, LANES),
@@ -272,7 +288,7 @@
             return carry
 
         lax.fori_loop(1, SECTIONS, deliver, 0)
-        chunk_at(other_ref, mine, HALO_ROWS, LANES)[...] = held[partner_ref[gz]]
+        chunk_at(other_ref, mine, HALO_ROWS, LANES)[...] = held[partner_ref[0, gz]]
 
     def side_copies(ref, slot):
         to_right = copy(
@@ -463,24 +479,29 @@
     slots_ref,
     info_ref,
     mask_ref,
-    place_ref,
-    rows_both,
-    row_sums,
-    columns_twice,
-    columns_low,
-    back_columns_high,
-    back_columns_low,
-    back_rows_high,
-    back_rows_low,
-    correlation_ref,
-    warped_ref,
-    strip,
-    spectra,
-    parts,
-    cells,
-    shifted,
-    canvas,
+    *rest,
 ):
+    tables_hbm, (correlation_hbm, warped_ref), rest = rest[:8], rest[8:10], rest[10:]
+    tables_vmem, (strip, spectra, parts, cells, shifted, canvas, result, table_sem, out_sem) = (
+        rest[:8],
+        rest[8:],
+    )
+    loads = [
+        pltpu.make_async_copy(src, dst, table_sem.at[index])
+        for index, (src, dst) in enumerate(zip(tables_hbm, tables_vmem))
+    ]
+    for load in loads:
+        load.start()
+    (
+        rows_both,
+        row_sums,
+        columns_twice,
+        columns_low,
+        back_columns_high,
+        back_columns_low,
+        back_rows_high,
+        back_rows_low,
+    ) = tables_vmem
     lane = lax.broadcasted_iota(jnp.int32, (PATCH_SIZE, LANES), 1)
     means, squares = [], []
     for index, ref in enumerate((own_ref, other_ref)):
@@ -498,6 +519,8 @@
             squares.append(jnp.sum(centred * centred, keepdims=True))
             strip[:, pl.ds((index * HALVES + block) * LANES, LANES)] = window.astype(bf16)
 
+    for load in loads:
+        load.wait()
     levels = [sum(means[:HALVES]) * (1.0 / HALVES), sum(means[HALVES:]) * (1.0 / HALVES)]
     for block in range(2 * HALVES):
         both = dot(rows_both[...], strip[:, pl.ds(block * LANES, LANES)])
@@ -526,6 +549,7 @@
         a = jnp.where(constant, 0.0, one(upper, low))
         return a, one(lower, high), one(lower, low), one(upper, high)
 
+    stores = []
     for patch in range(PATCH_COLS):
         scale = mask_ref[0, patch].astype(f32) * (1.0 / PATCH_SIZE**3)
         for base in (0, HALVES):
@@ -554,15 +578,19 @@
             + dot(high, back_columns_low[...])
         )
         high, low = split(half)
-        correlation_ref[patch] = (
+        result[patch] = (
             dot(back_rows_high[...], high)
             + dot(back_rows_high[...], low)
             + dot(back_rows_low[...], high)
         )
+        stores.append(
+            pltpu.make_async_copy(result.at[patch], correlation_hbm.at[patch], out_sem.at[patch])
+        )
+        stores[-1].start()
 
     cells[...] = jnp.zeros_like(cells)
     shifted[...] = jnp.zeros_like(shifted)
-    mine = place_ref[0] * 8
+    mine = (lax.axis_index("gy") * 4 + lax.axis_index("gx")) * 8
 
     def entry(index, carry):
         source, kind, rank = index // 4, index % 4 // 2, index % 2
@@ -598,22 +626,17 @@
             wide = pltpu.roll(wide, shift, 1)
         canvas[:, first : first + 2 * LANES] = canvas[:, first : first + 2 * LANES] + wide
     warped_ref[...] = canvas[:, LANES : LANES + WIDTH]
+    for store in stores:
+        store.wait()
 
 
 VMEM = pl.BlockSpec(memory_space=pltpu.VMEM)
 SMEM = pl.BlockSpec(memory_space=pltpu.SMEM)
+ANY = pl.BlockSpec(memory_space=pl.ANY)
 
 
 def body(tables, images, partner, patch_mask, flows, dest_count, dest_owner, dest_cell):
     tile = images[0]
-    fixed = jnp.round(flows.astype(f32) * float(2**FIXED)).astype(jnp.int32).reshape(16)
-    table = pl.pallas_call(
-        table_kernel,
-        out_shape=jax.ShapeDtypeStruct((1, 128), jnp.int32),
-        in_specs=[SMEM] * 4,
-        out_specs=SMEM,
-        scratch_shapes=[pltpu.SMEM((16,), jnp.int32)],
-    )(dest_owner.reshape(16), dest_cell.reshape(16), dest_count.reshape(8), fixed)
     own, other, slots, info = pl.pallas_call(
         exchange_kernel,
         out_shape=[
@@ -622,7 +645,7 @@
             jax.ShapeDtypeStruct((8, 4, HEIGHT, LANES), bf16),
             jax.ShapeDtypeStruct((8, 2, 1, 128), jnp.int32),
         ],
-        in_specs=[VMEM, SMEM, VMEM, SMEM],
+        in_specs=[VMEM, SMEM, SMEM, SMEM, SMEM, VMEM],
         out_specs=[VMEM] * 4,
         scratch_shapes=[
             pltpu.VMEM((SECTIONS, 16, LANES), bf16),
@@ -631,6 +654,9 @@
             pltpu.VMEM((2 * BLOCKS, HEIGHT, LANES), bf16),
             pltpu.VMEM((8, 4, HEIGHT, LANES), bf16),
             pltpu.VMEM((2, 1, 128), jnp.int32),
+            pltpu.VMEM((2, BLOCKS), jnp.int32),
+            pltpu.SMEM((2, BLOCKS), jnp.int32),
+            pltpu.SMEM((1, 128), jnp.int32),
             pltpu.SMEM((1, 128), jnp.int32),
             pltpu.SemaphoreType.DMA((2,)),
             pltpu.SemaphoreType.DMA((2,)),
@@ -639,28 +665,38 @@
             pltpu.SemaphoreType.DMA,
         ],
         compiler_params=pltpu.CompilerParams(
-            collective_id=0, has_side_effects=True, vmem_limit_bytes=24 * 2**20
+            collective_id=0, has_side_effects=True, vmem_limit_bytes=VMEM_BYTES
         ),
-    )(tile, partner.reshape(SECTIONS), table, table)
-    place = (lax.axis_index("gy") * 4 + lax.axis_index("gx")).astype(jnp.int32).reshape(1)
+    )(
+        tile,
+        partner[0],
+        dest_owner[0, 0, 0].T,
+        dest_cell[0, 0, 0].T,
+        dest_count[0, 0],
+        flows[0, 0, 0].T,
+    )
     correlation, warped = pl.pallas_call(
         compute_kernel,
         out_shape=[
             jax.ShapeDtypeStruct((PATCH_COLS, PATCH_SIZE, PATCH_SIZE), f32),
             jax.ShapeDtypeStruct((HEIGHT, WIDTH), f32),
         ],
-        in_specs=[VMEM, VMEM, VMEM, SMEM, SMEM, SMEM] + [VMEM] * 8,
-        out_specs=[VMEM] * 2,
-        scratch_shapes=[
+        in_specs=[VMEM, VMEM, VMEM, SMEM, SMEM] + [ANY] * 8,
+        out_specs=[ANY, VMEM],
+        scratch_shapes=[pltpu.VMEM(table.shape, table.dtype) for table in tables]
+        + [
             pltpu.VMEM((PATCH_SIZE, 2 * HALVES * LANES), bf16),
             pltpu.VMEM((2 * HALVES, 2 * WAVES, 2 * LANES), bf16),
             pltpu.VMEM((2 * HALVES, 2 * WAVES, 2 * LANES), f32),
             pltpu.VMEM((BLOCKS, HEIGHT, LANES), f32),
             pltpu.VMEM((128, LANES), f32),
             pltpu.VMEM((HEIGHT, STRIP_COLS), f32),
+            pltpu.VMEM((PATCH_COLS, PATCH_SIZE, PATCH_SIZE), f32),
+            pltpu.SemaphoreType.DMA((8,)),
+            pltpu.SemaphoreType.DMA((PATCH_COLS,)),
         ],
-        compiler_params=pltpu.CompilerParams(vmem_limit_bytes=40 * 2**20),
-    )(own, other, slots, info, patch_mask[0], place, *tables)
+        compiler_params=pltpu.CompilerParams(vmem_limit_bytes=VMEM_BYTES),
+    )(own, other, slots, info, patch_mask[0], *tables)
     return correlation[None, None], warped[None]
 
 

time: 80.5 us -> 67.7 us (0.84)
  local copies, waits for them, and re-layouts: 13.4 us -> 0 us
  Pallas kernels: 65.3 us -> 66.9 us
    unnamed x26 -> x0, local copies, waits for them, and re-layouts: 11.5 us -> none
    reshape x3 -> x0, local copies, waits for them, and re-layouts: 1.81 us -> none  [the longest x1 0.63 us: body(): jnp.round(flows.astype(f32) * float(2 ** FIXED)).astype(jnp.int32)]
    pallas_call x1, Pallas kernels: 11.3 us -> 12.8 us  [body(): pl.pallas_call(compute_kernel, out_shape=[jax.ShapeDtypeStruct((PATCH_COL...]
    pallas_call x1, Pallas kernels: 52.6 us -> 54.1 us  [body(): pl.pallas_call(exchange_kernel, out_shape=[jax.ShapeDtypeStruct((STRIP_RO...]
    pallas_call x1 -> x0, Pallas kernels: 1.39 us -> none  [body(): pl.pallas_call(table_kernel, out_shape=jax.ShapeDtypeStruct((1, 128), jnp...]
where the time goes in v1:
time: 67.7 us; the launch traced here: 67.5 us
  Pallas kernels  66.9 us (99%)
    pallas_call x1, Pallas kernels, body(): pl.pallas_call(exchange_kernel, out_shape=[jax.ShapeDtypeStruct((STRIP_RO...  54.1 us
    pallas_call x1, Pallas kernels, body(): pl.pallas_call(compute_kernel, out_shape=[jax.ShapeDtypeStruct((PATCH_COL...  12.8 us

profile of v1, /device:TPU:1, one launch (start us, length us, event | category | flops | bytes accessed | tf_op | source)
XLA Modules:
  0.0 67.5 jit_solution(7291865239408327934)
XLA Ops:
  0.6 54.1 %shard_map.158 = (bf16[176,896]{1,0:T(8,128)(2,1)}, bf16[176,896]{1,0:T(8,128)(2,1)}, bf16[8,4,80,128]{3,2,1,0:T(8,128)(2,1)}, s32[8,2,1,128]{3,2,1,0:T(1,128)}) custom-call(bf16[80,640]{1,0:T(8,128)(2,1)} %bitcast.15, s32[1,32]{1,0:T(1,128)} %bitcast.18, s32[2,8]{1,0:T(2,128)} %bitcast.16, s32[2,8]{1,0:T(2,128)} %bitcast.17, s32[1,8]{1,0:T(1,128)} %bitcast.19, ...), custom_call_target="tpu_custom_call" | custom-call | tf_op jit(solution)/shard_map/pallas_call | solution.py:640
  54.7 12.8 %shard_map.159 = (f32[8,160,160]{2,1,0:T(8,128)}, f32[80,640]{1,0:T(8,128)}) custom-call(bf16[176,896]{1,0:T(8,128)(2,1)} %get-tuple-element.8.own_ref, bf16[176,896]{1,0:T(8,128)(2,1)} %get-tuple-element.9.other_ref, bf16[8,4,80,128]{3,2,1,0:T(8,128)(2,1)} %get-tuple-element.10.slots_ref, s32[8,2,1,128]{3,2,1,0:T(1,128)} %get-tuple-element.11.info_ref, ...), custom_call_target="tpu_custom_call" | custom-call | tf_op jit(solution)/shard_map/pallas_call | solution.py:678

commit v2 on v1

v2 whole, which is shorter than its diff:
```python
import functools

import jax
import jax.numpy as jnp
import ml_dtypes
import numpy as np
from jax import lax
from jax.experimental import pallas as pl
from jax.experimental.pallas import tpu as pltpu
from jax.sharding import PartitionSpec as P

PATCH_SIZE = 160
STRIDE = 80
PATCH_COLS = 8
MARGIN = 24
DEST_SLOTS = 2
BLOCKS = 8
OWNERS = 16
PADDED = 128
SECTIONS = 32
HEIGHT = 80
WIDTH = 640
CHUNKS = 25
LANES = 128
HALO_ROWS = 48
STRIP_ROWS = HEIGHT + 2 * HALO_ROWS
STRIP_COLS = WIDTH + 2 * LANES
HALVES = 9
WAVES = 88
VMEM_BYTES = 60 * 2**20
FIXED = 24

epsilon = 1e-05
f32 = jnp.float32
bf16 = jnp.bfloat16
MESH = pl.DeviceIdType.MESH


def halves(table):
    high = table.astype(ml_dtypes.bfloat16)
    low = (table - high.astype(np.float64)).astype(ml_dtypes.bfloat16)
    return high, low


def make_tables():
    wave = np.arange(81)
    place = np.arange(PATCH_SIZE)
    angle = 2.0 * np.pi * (np.outer(wave, place) % PATCH_SIZE) / PATCH_SIZE
    cosine, sine = np.cos(angle), np.sin(angle)
    sine[0] = 0.0
    sine[80] = 0.0
    rows = np.zeros((2 * WAVES, PATCH_SIZE))
    rows[:81] = cosine
    rows[WAVES : WAVES + 81] = sine
    rows_high, rows_low = halves(rows)
    rows_both = np.concatenate([rows_high, rows_low], axis=0)
    row_sums = (rows_high.astype(np.float64) + rows_low.astype(np.float64)).sum(axis=1)
    row_sums = np.broadcast_to(row_sums[:, None], (2 * WAVES, LANES)).astype(np.float32)
    columns = np.zeros((LANES, 2 * LANES))
    columns[:STRIDE, :81] = cosine[:, :STRIDE].T
    columns[:STRIDE, LANES : LANES + 81] = sine[:, :STRIDE].T
    columns_high, columns_low = halves(columns)
    columns_twice = np.concatenate([columns_high, columns_high], axis=0)
    weight = np.ones(81)
    weight[0] = weight[80] = 0.5
    back_columns = np.zeros((2 * LANES, PATCH_SIZE))
    back_columns[:81] = weight[:, None] * cosine
    back_columns[LANES : LANES + 81] = weight[:, None] * sine
    back_columns = halves(back_columns)
    weight = np.full(81, 2.0)
    weight[0] = weight[80] = 1.0
    back_rows = np.zeros((PATCH_SIZE, 2 * WAVES))
    back_rows[:, :81] = (weight[:, None] * cosine).T
    back_rows[:, WAVES : WAVES + 81] = -(weight[:, None] * sine).T
    back_rows = halves(back_rows)
    return (rows_both, row_sums, columns_twice, columns_low, *back_columns, *back_rows)


def fill_table(owner_ref, cell_ref, count_ref, flow_ref, table_ref):
    owners, codes = [], []
    for block in range(BLOCKS):
        for entry in range(DEST_SLOTS):
            live = entry < count_ref[0, block]
            owners.append(jnp.where(live, owner_ref[entry, block], -1))
            codes.append(BLOCKS * block + cell_ref[entry, block])

    def one(owner, carry):
        first = second = jnp.int32(-1)
        for named, code in zip(owners, codes):
            match = named == owner
            second = jnp.where(match, first, second)
            first = jnp.where(match, code, first)
        for rank, code in enumerate((first, second)):
            block = jnp.maximum(code, 0) >> 3
            base = 8 * owner + 4 * rank
            table_ref[0, base] = block
            table_ref[0, base + 1] = jnp.where(code < 0, -1, code & 7)
            table_ref[0, base + 2] = flow_ref[0, block]
            table_ref[0, base + 3] = flow_ref[1, block]
        return carry

    lax.fori_loop(0, OWNERS, one, 0)


def chunk_of(index):
    line, place = index // 8, index % 8
    holds = ((place >= 1) & (place <= 6)) | (index == 0)
    return holds, jnp.where(index == 0, CHUNKS - 1, line * 6 + place - 1)


def holder_of(chunk):
    return jnp.where(chunk == CHUNKS - 1, 0, (chunk // 6) * 8 + chunk % 6 + 1)


def chunk_at(ref, chunk, row, column):
    rows = pl.ds(pl.multiple_of(row + 16 * (chunk // 5), 16), 16)
    columns = pl.ds(pl.multiple_of(column + LANES * (chunk % 5), LANES), LANES)
    return ref.at[rows, columns]


def exchange_kernel(
    tile_ref,
    partner_ref,
    owner_ref,
    cell_ref,
    count_ref,
    flow_ref,
    *rest,
):
    tables_hbm, (other_ref, parts_hbm, warped_hbm, scale_ref), rest = rest[:4], rest[4:8], rest[8:]
    tables_vmem, rest = rest[:4], rest[4:]
    (
        own_ref,
        slots_ref,
        info_ref,
        info_smem,
        held,
        sorted_,
        mirror,
        blocks,
        outgoing,
        tables,
        fixed,
        fixed_smem,
        table_smem,
        mirror_smem,
        strip,
        spectra,
        parts,
        cells,
        shifted,
        canvas,
        warped,
        send_sem,
        recv_sem,
        far_sem,
        slot_sem,
        local_sem,
        table_sem,
        out_sem,
    ) = rest
    gz, gy, gx = lax.axis_index("gz"), lax.axis_index("gy"), lax.axis_index("gx")
    half, core = gy // 2, gy % 2
    place = core * 4 + gx
    far_gy = 3 - gy
    near_gy = gy + 1 - 2 * core

    barrier = pltpu.get_barrier_semaphore()

    def greet(step, carry):
        pl.semaphore_signal(
            barrier, inc=1, device_id={"gz": lax.rem(gz + step, SECTIONS)}, device_id_type=MESH
        )
        return carry

    pl.semaphore_signal(barrier, inc=1, device_id={"gy": far_gy}, device_id_type=MESH)
    lax.fori_loop(1, SECTIONS, greet, 0)
    for step in range(1, 8):
        other_place = lax.rem(place + step, 8)
        pl.semaphore_signal(
            barrier,
            inc=1,
            device_id={"gy": 2 * half + other_place // 4, "gx": other_place % 4},
            device_id_type=MESH,
        )

    loads = [
        pltpu.make_async_copy(src, dst, table_sem.at[index])
        for index, (src, dst) in enumerate(zip(tables_hbm, tables_vmem))
    ]
    for load in loads:
        load.start()
    fixed[...] = jnp.round(flow_ref[...].astype(f32) * float(2**FIXED)).astype(jnp.int32)
    to_scalars = pltpu.make_async_copy(fixed, fixed_smem, local_sem)
    to_scalars.start()
    own_ref[pl.ds(HALO_ROWS, HEIGHT), pl.ds(LANES, WIDTH)] = tile_ref[...]
    top, bottom = pl.ds(0, HALO_ROWS), pl.ds(HALO_ROWS + HEIGHT, HALO_ROWS)
    left, right = pl.ds(0, LANES), pl.ds(LANES + WIDTH, LANES)
    middle = pl.ds(LANES, WIDTH)
    for ref in (own_ref, other_ref):

        @pl.when(gy == 0)
        def _():
            ref[top, middle] = jnp.zeros((HALO_ROWS, WIDTH), bf16)

        @pl.when(gy == 3)
        def _():
            ref[bottom, middle] = jnp.zeros((HALO_ROWS, WIDTH), bf16)

        @pl.when(gx == 0)
        def _():
            ref[:, left] = jnp.zeros((STRIP_ROWS, LANES), bf16)

        @pl.when(gx == 3)
        def _():
            ref[:, right] = jnp.zeros((STRIP_ROWS, LANES), bf16)

    lane = lax.broadcasted_iota(jnp.int32, (HEIGHT, LANES), 1)

    def cut_blocks(ref, base):
        for block in range(BLOCKS):
            start = STRIDE * block
            first = start // LANES * LANES
            shift = start - first
            width = LANES if shift + STRIDE <= LANES else 2 * LANES
            window = ref[:, first : first + width].astype(f32)
            if shift:
                window = pltpu.roll(window, width - shift, 1)[:, :LANES]
            blocks[base + block] = jnp.where(lane < STRIDE, window, 0.0).astype(bf16)

    def fill(kind, table):
        for target in range(8):
            base = 8 * (8 * half + target)
            for rank in range(2):
                block = table[0, base + 4 * rank]
                outgoing[kind, target, rank] = blocks[BLOCKS * kind + block]

    cut_blocks(tile_ref, 0)
    to_scalars.wait()
    fill_table(owner_ref, cell_ref, count_ref, fixed_smem, table_smem)
    to_vector = pltpu.make_async_copy(table_smem, tables.at[0], local_sem)
    to_vector.start()
    fill(0, table_smem)
    to_vector.wait()
    holds, mine = chunk_of(gz)
    pl.semaphore_wait(barrier, SECTIONS - 1 + 8)

    def scatter(step, carry):
        chunk = lax.rem(mine + step, CHUNKS)
        holder = holder_of(chunk)

        @pl.when(holder != gz)
        def _():
            pltpu.make_async_remote_copy(
                src_ref=chunk_at(tile_ref, chunk, 0, 0),
                dst_ref=held.at[gz],
                send_sem=send_sem.at[0],
                recv_sem=recv_sem.at[0],
                device_id={"gz": holder},
                device_id_type=MESH,
            ).start()

        return carry

    def copy(src, dst, slot, device):
        return pltpu.make_async_remote_copy(
            src_ref=src,
            dst_ref=dst,
            send_sem=far_sem.at[0, slot],
            recv_sem=far_sem.at[1, slot],
            device_id=device,
            device_id_type=MESH,
        )

    near = {"gy": near_gy}
    own_down = copy(
        tile_ref.at[pl.ds(HEIGHT - HALO_ROWS, HALO_ROWS), :], own_ref.at[top, middle], 0, near
    )
    own_up = copy(tile_ref.at[pl.ds(0, HALO_ROWS), :], own_ref.at[bottom, middle], 0, near)
    to_far = copy(tile_ref, mirror, 1, {"gy": far_gy})
    table_far = copy(tables.at[0], tables.at[1], 2, {"gy": far_gy})

    def send_slots(kind):
        def one(step, carry):
            target = lax.rem(place + step, 8)
            device = {"gy": 2 * half + target // 4, "gx": target % 4}
            for src, dst, row in (
                (outgoing.at[kind, target], slots_ref.at[kind, place], 0),
                (tables.at[kind], info_ref.at[kind, place], 1),
            ):
                pltpu.make_async_remote_copy(
                    src_ref=src,
                    dst_ref=dst,
                    send_sem=slot_sem.at[0, kind, row],
                    recv_sem=slot_sem.at[1, kind, row],
                    device_id=device,
                    device_id_type=MESH,
                ).start()
            return carry

        lax.fori_loop(1, 8, one, 0)
        slots_ref[kind, place] = outgoing[kind, place]
        info_ref[kind, place] = tables[kind]

    table_far.start()
    to_far.start()
    lax.fori_loop(0, CHUNKS, scatter, 0)

    @pl.when(core == 0)
    def _():
        own_down.start()

    @pl.when(core == 1)
    def _():
        own_up.start()

    send_slots(0)

    @pl.when(holds)
    def _():
        held[gz] = chunk_at(tile_ref, mine, 0, 0)[...]
        pltpu.make_async_copy(
            held.at[pl.ds(0, SECTIONS - 1)], held.at[pl.ds(0, SECTIONS - 1)], recv_sem.at[0]
        ).wait()
        for section in range(SECTIONS):
            sorted_[section] = held[partner_ref[0, section]]

        def deliver(step, carry):
            section = lax.rem(gz + step, SECTIONS)
            pltpu.make_async_remote_copy(
                src_ref=sorted_.at[section],
                dst_ref=chunk_at(other_ref, mine, HALO_ROWS, LANES),
                send_sem=send_sem.at[1],
                recv_sem=recv_sem.at[1],
                device_id={"gz": section},
                device_id_type=MESH,
            ).start()
            return carry

        lax.fori_loop(1, SECTIONS, deliver, 0)
        chunk_at(other_ref, mine, HALO_ROWS, LANES)[...] = sorted_[gz]


    def side_copies(ref, slot):
        to_right = copy(
            ref.at[:, pl.ds(WIDTH, LANES)], ref.at[:, left], slot, {"gx": jnp.minimum(gx + 1, 3)}
        )
        to_left = copy(
            ref.at[:, pl.ds(LANES, LANES)], ref.at[:, right], slot + 1, {"gx": jnp.maximum(gx - 1, 0)}
        )
        return to_right, to_left

    def start_sides(copies):
        @pl.when(gx < 3)
        def _():
            copies[0].start()

        @pl.when(gx > 0)
        def _():
            copies[1].start()

    def receive_sides(copies):
        @pl.when(gx > 0)
        def _():
            copies[0].wait_recv()

        @pl.when(gx < 3)
        def _():
            copies[1].wait_recv()

    def sent_sides(copies):
        @pl.when(gx < 3)
        def _():
            copies[0].wait_send()

        @pl.when(gx > 0)
        def _():
            copies[1].wait_send()

    chunks = held.at[pl.ds(0, CHUNKS)]
    fewer = held.at[pl.ds(0, CHUNKS - 1)]
    rows_up = pl.ds(HALO_ROWS, HALO_ROWS)
    rows_down = pl.ds(HEIGHT, HALO_ROWS)
    other_down = copy(
        other_ref.at[rows_down, middle], other_ref.at[top, middle], 5, {"gy": jnp.minimum(gy + 1, 3)}
    )
    other_up = copy(
        other_ref.at[rows_up, middle], other_ref.at[bottom, middle], 6, {"gy": jnp.maximum(gy - 1, 0)}
    )
    other_sides = side_copies(other_ref, 7)
    own_sides = side_copies(own_ref, 3)

    def pass_rows():
        @pl.when(holds)
        def _():
            pltpu.make_async_copy(fewer, fewer, recv_sem.at[1]).wait()

        @pl.when(jnp.logical_not(holds))
        def _():
            pltpu.make_async_copy(chunks, chunks, recv_sem.at[1]).wait()

        @pl.when(gy < 3)
        def _():
            other_down.start()

        @pl.when(gy > 0)
        def _():
            other_up.start()

    def pass_columns():
        @pl.when(gy > 0)
        def _():
            other_down.wait_recv()

        @pl.when(gy < 3)
        def _():
            other_up.wait_recv()

        start_sides(other_sides)

    def take_mirror():
        @pl.when(core == 1)
        def _():
            own_down.wait_recv()

        @pl.when(core == 0)
        def _():
            own_up.wait_recv()

        table_far.wait_recv()
        fetch = pltpu.make_async_copy(tables.at[1], mirror_smem, local_sem)
        fetch.start()
        to_far.wait_recv()

        @pl.when(gy == 1)
        def _():
            own_ref[bottom, middle] = mirror[pl.ds(0, HALO_ROWS), :]

        @pl.when(gy == 2)
        def _():
            own_ref[top, middle] = mirror[pl.ds(HEIGHT - HALO_ROWS, HALO_ROWS), :]

        start_sides(own_sides)
        cut_blocks(mirror, BLOCKS)
        fetch.wait()
        fill(1, mirror_smem)
        send_slots(1)

    stores = [
        pltpu.make_async_copy(parts, parts_hbm, out_sem.at[0]),
        pltpu.make_async_copy(warped, warped_hbm, out_sem.at[1]),
    ]

    def own_spectra():
        receive_sides(own_sides)
        for load in loads:
            load.wait()
        scales = forward(own_ref, strip, spectra, parts, *tables_vmem)
        stores[0].start()
        for patch, scale in enumerate(scales):
            scale_ref[patch : patch + 1, :] = jnp.broadcast_to(scale, (1, LANES))

    def warp():
        for kind in range(2):
            seven, seven_info = slots_ref.at[kind, pl.ds(0, 7)], info_ref.at[kind, pl.ds(0, 7)]
            pltpu.make_async_copy(seven, seven, slot_sem.at[1, kind, 0]).wait()
            pltpu.make_async_copy(seven_info, seven_info, slot_sem.at[1, kind, 1]).wait()
        fetch = pltpu.make_async_copy(info_ref, info_smem, local_sem)
        fetch.start()
        cells[...] = jnp.zeros_like(cells)
        shifted[...] = jnp.zeros_like(shifted)
        fetch.wait()
        add_up(slots_ref, info_smem, 8 * (4 * gy + gx), cells, shifted, canvas, warped)
        stores[1].start()

    take_mirror()
    own_spectra()
    pass_rows()
    warp()
    pass_columns()
    receive_sides(other_sides)

    for kind in range(2):
        seven, seven_info = slots_ref.at[kind, pl.ds(0, 7)], info_ref.at[kind, pl.ds(0, 7)]
        pltpu.make_async_copy(seven, seven, slot_sem.at[0, kind, 0]).wait()
        pltpu.make_async_copy(seven_info, seven_info, slot_sem.at[0, kind, 1]).wait()

    @pl.when(holds)
    def _():
        pltpu.make_async_copy(fewer, fewer, send_sem.at[0]).wait()
        all_but_one = held.at[pl.ds(0, SECTIONS - 1)]
        pltpu.make_async_copy(all_but_one, all_but_one, send_sem.at[1]).wait()

    @pl.when(jnp.logical_not(holds))
    def _():
        pltpu.make_async_copy(chunks, chunks, send_sem.at[0]).wait()

    @pl.when(core == 0)
    def _():
        own_down.wait_send()

    @pl.when(core == 1)
    def _():
        own_up.wait_send()

    to_far.wait_send()
    table_far.wait_send()

    @pl.when(gy < 3)
    def _():
        other_down.wait_send()

    @pl.when(gy > 0)
    def _():
        other_up.wait_send()

    sent_sides(own_sides)
    sent_sides(other_sides)
    for store in stores:
        store.wait()


def split(value):
    high = value.astype(bf16)
    return high, (value - high.astype(f32)).astype(bf16)


def dot(left, right):
    return jnp.dot(left, right, preferred_element_type=f32)


def forward(ref, strip, spectra, parts, rows_both, row_sums, columns_twice, columns_low):
    lane = lax.broadcasted_iota(jnp.int32, (PATCH_SIZE, LANES), 1)
    means, squares = [], []
    for block in range(HALVES):
        start = LANES - 40 + STRIDE * block
        first = start // LANES * LANES
        shift = start - first
        width = LANES if shift + STRIDE <= LANES else 2 * LANES
        window = ref[8 : 8 + PATCH_SIZE, first : first + width].astype(f32)
        window = pltpu.roll(window, width - shift, 1)[:, :LANES]
        window = jnp.where(lane < STRIDE, window, 0.0)
        mean = jnp.sum(window, keepdims=True) * (1.0 / (PATCH_SIZE * STRIDE))
        centred = jnp.where(lane < STRIDE, window - mean, 0.0)
        means.append(mean)
        squares.append(jnp.sum(centred * centred, keepdims=True))
        strip[:, pl.ds(block * LANES, LANES)] = window.astype(bf16)

    level = sum(means) * (1.0 / HALVES) * row_sums[...]
    for block in range(HALVES):
        both = dot(rows_both[...], strip[:, pl.ds(block * LANES, LANES)])
        value = both[: 2 * WAVES] + both[2 * WAVES :] - level
        high, low = split(value)
        spectra[block, :, :LANES] = high
        spectra[block, :, LANES:] = low
    for block in range(HALVES):
        parts[block] = dot(spectra[block], columns_twice[...]) + dot(
            spectra[block, :, :LANES], columns_low[...]
        )

    count = PATCH_SIZE * STRIDE
    scales = []
    for patch in range(PATCH_COLS):
        gap = means[patch] - means[patch + 1]
        spread = (squares[patch] + squares[patch + 1] + gap * gap * (count / 2)) * (0.5 / count)
        scales.append(1.0 / jnp.sqrt(spread + epsilon))
    return scales


def add_up(slots_ref, info_smem, mine, cells, shifted, canvas, warped):
    unit = 1.0 / 2**FIXED

    def entries(source, carry):
        values, named = [], []
        for kind in range(2):
            for rank in range(2):
                base = mine + 4 * rank
                named.append(info_smem[kind, source, 0, base + 1])
                down = info_smem[kind, source, 0, base + 2]
                across = info_smem[kind, source, 0, base + 3]
                whole_down = jnp.clip(down >> FIXED, 1 - MARGIN, MARGIN - 1)
                whole_across = jnp.clip(across >> FIXED, 1 - MARGIN, MARGIN - 1)
                part_down = (down & (2**FIXED - 1)).astype(f32) * unit
                part_across = (across & (2**FIXED - 1)).astype(f32) * unit
                block = slots_ref[kind, source, rank].astype(f32)
                here = pltpu.roll(block, whole_across + MARGIN, 1)
                after = pltpu.roll(here, 1, 1)
                room = shifted.at[2 * kind + rank]
                room[pl.ds(MARGIN, HEIGHT), :] = here * (1.0 - part_across) + after * part_across
                here = room[pl.ds(MARGIN - whole_down, HEIGHT), :]
                after = room[pl.ds(MARGIN - 1 - whole_down, HEIGHT), :]
                value = here * (1.0 - part_down) + after * part_down
                values.append(value.astype(bf16).astype(f32))
        for cell in range(BLOCKS):
            total = cells[cell]
            for value, name in zip(values, named):
                total = total + value * (name == cell).astype(f32)
            cells[cell] = total
        return carry

    lax.fori_loop(0, 8, entries, 0)
    canvas[...] = jnp.zeros_like(canvas)
    for cell in range(BLOCKS):
        start = LANES - MARGIN + STRIDE * cell
        first = start // LANES * LANES
        shift = start - first
        wide = jnp.concatenate([cells[cell], jnp.zeros((HEIGHT, LANES), f32)], axis=1)
        if shift:
            wide = pltpu.roll(wide, shift, 1)
        canvas[:, first : first + 2 * LANES] = canvas[:, first : first + 2 * LANES] + wide
    warped[...] = canvas[:, LANES : LANES + WIDTH]


def compute_kernel(other_ref, parts_hbm, warped_in, scale_ref, mask_ref, *rest):
    tables_hbm, (correlation_hbm, warped_hbm), rest = rest[:8], rest[8:10], rest[10:]
    tables_vmem, rest = rest[:8], rest[8:]
    strip, spectra, own_parts, parts, result, table_sem, part_sem, out_sem = rest
    loads = [
        pltpu.make_async_copy(src, dst, table_sem.at[index])
        for index, (src, dst) in enumerate(zip(tables_hbm, tables_vmem))
    ]
    for load in loads:
        load.start()
    own_load = pltpu.make_async_copy(parts_hbm, own_parts, part_sem)
    own_load.start()
    stores = [pltpu.make_async_copy(warped_in, warped_hbm, out_sem.at[PATCH_COLS])]
    stores[0].start()
    back_columns_high, back_columns_low, back_rows_high, back_rows_low = tables_vmem[4:]
    for load in loads:
        load.wait()
    scales = forward(other_ref, strip, spectra, parts, *tables_vmem[:4])
    own_load.wait()

    row = lax.broadcasted_iota(jnp.int32, (WAVES, LANES), 0)
    column = lax.broadcasted_iota(jnp.int32, (WAVES, LANES), 1)
    constant = (row == 0) & (column == 0)
    odd = column % 2 == 1

    def spectrum(ref, first):
        def one(rows, lanes):
            later = ref[first + 1, rows, lanes]
            return ref[first, rows, lanes] + jnp.where(odd, -later, later)

        upper, lower = pl.ds(0, WAVES), pl.ds(WAVES, WAVES)
        low, high = pl.ds(0, LANES), pl.ds(LANES, LANES)
        a = jnp.where(constant, 0.0, one(upper, low))
        return a, one(lower, high), one(lower, low), one(upper, high)

    for patch in range(PATCH_COLS):
        scale = mask_ref[0, patch].astype(f32) * (2.0 / PATCH_SIZE**3)
        scale = scale * scales[patch] * scale_ref[patch : patch + 1, :]
        a, b, c, d = spectrum(own_parts, patch)
        e, f, g, h = spectrum(parts, patch)
        even_real = (a * e + b * f + c * g + d * h) * scale
        odd_real = (c * h + d * g - a * f - b * e) * scale
        even_imag = (c * e - d * f - a * g + b * h) * scale
        odd_imag = (d * e - c * f - a * h + b * g) * scale
        joined = jnp.concatenate(
            [
                jnp.concatenate([even_real, -odd_imag], axis=1),
                jnp.concatenate([even_imag, odd_real], axis=1),
            ],
            axis=0,
        )
        high, low = split(joined)
        half = (
            dot(high, back_columns_high[...])
            + dot(low, back_columns_high[...])
            + dot(high, back_columns_low[...])
        )
        high, low = split(half)
        result[patch] = (
            dot(back_rows_high[...], high)
            + dot(back_rows_high[...], low)
            + dot(back_rows_low[...], high)
        )
        stores.append(
            pltpu.make_async_copy(result.at[patch], correlation_hbm.at[patch], out_sem.at[patch])
        )
        stores[-1].start()
    for store in stores:
        store.wait()


VMEM = pl.BlockSpec(memory_space=pltpu.VMEM)
SMEM = pl.BlockSpec(memory_space=pltpu.SMEM)
ANY = pl.BlockSpec(memory_space=pl.ANY)


def body(tables, images, partner, patch_mask, flows, dest_count, dest_owner, dest_cell):
    space = [pltpu.VMEM(table.shape, table.dtype) for table in tables]
    parts_shape = (HALVES, 2 * WAVES, 2 * LANES)
    other, parts, warped, scale = pl.pallas_call(
        exchange_kernel,
        out_shape=[
            jax.ShapeDtypeStruct((STRIP_ROWS, STRIP_COLS), bf16),
            jax.ShapeDtypeStruct(parts_shape, f32),
            jax.ShapeDtypeStruct((HEIGHT, WIDTH), f32),
            jax.ShapeDtypeStruct((PATCH_COLS, LANES), f32),
        ],
        in_specs=[VMEM, SMEM, SMEM, SMEM, SMEM, VMEM] + [ANY] * 4,
        out_specs=[VMEM, ANY, ANY, VMEM],
        scratch_shapes=space[:4]
        + [
            pltpu.VMEM((STRIP_ROWS, STRIP_COLS), bf16),
            pltpu.VMEM((2, 8, 2, HEIGHT, LANES), bf16),
            pltpu.VMEM((2, 8, 1, 128), jnp.int32),
            pltpu.SMEM((2, 8, 1, 128), jnp.int32),
            pltpu.VMEM((SECTIONS, 16, LANES), bf16),
            pltpu.VMEM((SECTIONS, 16, LANES), bf16),
            pltpu.VMEM((HEIGHT, WIDTH), bf16),
            pltpu.VMEM((2 * BLOCKS, HEIGHT, LANES), bf16),
            pltpu.VMEM((2, 8, 2, HEIGHT, LANES), bf16),
            pltpu.VMEM((2, 1, 128), jnp.int32),
            pltpu.VMEM((2, BLOCKS), jnp.int32),
            pltpu.SMEM((2, BLOCKS), jnp.int32),
            pltpu.SMEM((1, 128), jnp.int32),
            pltpu.SMEM((1, 128), jnp.int32),
            pltpu.VMEM((PATCH_SIZE, HALVES * LANES), bf16),
            pltpu.VMEM(parts_shape, bf16),
            pltpu.VMEM(parts_shape, f32),
            pltpu.VMEM((BLOCKS, HEIGHT, LANES), f32),
            pltpu.VMEM((4, 128, LANES), f32),
            pltpu.VMEM((HEIGHT, STRIP_COLS), f32),
            pltpu.VMEM((HEIGHT, WIDTH), f32),
            pltpu.SemaphoreType.DMA((2,)),
            pltpu.SemaphoreType.DMA((2,)),
            pltpu.SemaphoreType.DMA((2, 9)),
            pltpu.SemaphoreType.DMA((2, 2, 2)),
            pltpu.SemaphoreType.DMA,
            pltpu.SemaphoreType.DMA((4,)),
            pltpu.SemaphoreType.DMA((2,)),
        ],
        compiler_params=pltpu.CompilerParams(
            collective_id=0, has_side_effects=True, vmem_limit_bytes=VMEM_BYTES
        ),
    )(
        images[0],
        partner[0],
        dest_owner[0, 0, 0].T,
        dest_cell[0, 0, 0].T,
        dest_count[0, 0],
        flows[0, 0, 0].T,
        *tables[:4],
    )
    correlation, warped = pl.pallas_call(
        compute_kernel,
        out_shape=[
            jax.ShapeDtypeStruct((PATCH_COLS, PATCH_SIZE, PATCH_SIZE), f32),
            jax.ShapeDtypeStruct((HEIGHT, WIDTH), f32),
        ],
        in_specs=[VMEM, ANY, ANY, VMEM, SMEM] + [ANY] * 8,
        out_specs=[ANY, ANY],
        scratch_shapes=space
        + [
            pltpu.VMEM((PATCH_SIZE, HALVES * LANES), bf16),
            pltpu.VMEM(parts_shape, bf16),
            pltpu.VMEM(parts_shape, f32),
            pltpu.VMEM(parts_shape, f32),
            pltpu.VMEM((PATCH_COLS, PATCH_SIZE, PATCH_SIZE), f32),
            pltpu.SemaphoreType.DMA((8,)),
            pltpu.SemaphoreType.DMA,
            pltpu.SemaphoreType.DMA((PATCH_COLS + 1,)),
        ],
        compiler_params=pltpu.CompilerParams(vmem_limit_bytes=VMEM_BYTES),
    )(other, parts, warped, scale, patch_mask[0], *tables)
    return correlation[None, None], warped[None]


def solution(mesh):
    placed = (
        P("gz", "gy", "gx"),
        P("gy", "gx", None),
        P("gz", "gy", "gx"),
        P("gz", "gy", "gx", None, None),
        P("gz", "gy", "gx", None),
        P("gz", "gy", "gx", None, None),
        P("gz", "gy", "gx", None, None),
    )
    tables = tuple(jnp.asarray(table) for table in make_tables())
    return jax.shard_map(
        functools.partial(body, tables),
        mesh=mesh,
        in_specs=placed,
        out_specs=(P("gz", "gy", "gx", None, None), P("gz", "gy", "gx")),
        check_vma=False,
    )
```

time: 67.7 us -> 61.4 us (0.907)
  Pallas kernels: 66.9 us -> 60.6 us
    pallas_call x1, Pallas kernels: 12.8 us -> 8.47 us  [body(): pl.pallas_call(compute_kernel, out_shape=[jax.ShapeDtypeStruct((PATCH_COL...]
    pallas_call x1, Pallas kernels: 54.1 us -> 52.1 us  [body(): pl.pallas_call(exchange_kernel, out_shape=[jax.ShapeDtypeStruct((STRIP_RO...]
where the time goes in v2:
time: 61.4 us; the launch traced here: 61.3 us
  Pallas kernels  60.6 us (99%)
  between operations  0.64 us (1%)
    pallas_call x1, Pallas kernels, body(): pl.pallas_call(exchange_kernel, out_shape=[jax.ShapeDtypeStruct((STRIP_RO...  52.1 us
    pallas_call x1, Pallas kernels, body(): pl.pallas_call(compute_kernel, out_shape=[jax.ShapeDtypeStruct((PATCH_COL...  8.47 us

profile of v2, /device:TPU:1, one launch (start us, length us, event | category | flops | bytes accessed | tf_op | source)
XLA Modules:
  0.0 61.3 jit_solution(12104406889807452710)
XLA Ops:
  0.6 52.1 %shard_map.158 = (bf16[176,896]{1,0:T(8,128)(2,1)}, f32[9,176,256]{2,1,0:T(8,128)}, f32[80,640]{1,0:T(8,128)}, f32[8,128]{1,0:T(8,128)}) custom-call(bf16[80,640]{1,0:T(8,128)(2,1)} %bitcast.15, s32[1,32]{1,0:T(1,128)} %bitcast.19, s32[2,8]{1,0:T(2,128)} %bitcast.16, s32[2,8]{1,0:T(2,128)} %bitcast.17, s32[1,8]{1,0:T(1,128)} %bitcast.20, ...), custom_call_target="tpu_custom_call" | custom-call | tf_op jit(solution)/shard_map/pallas_call | solution.py:693
  52.8 8.5 %shard_map.159 = (f32[8,160,160]{2,1,0:T(8,128)}, f32[80,640]{1,0:T(8,128)}) custom-call(bf16[176,896]{1,0:T(8,128)(2,1)} %get-tuple-element.8.other_ref, f32[9,176,256]{2,1,0:T(8,128)} %get-tuple-element.9.parts_hbm, f32[80,640]{1,0:T(8,128)} %get-tuple-element.10.warped_in, f32[8,128]{1,0:T(8,128)} %get-tuple-element.11.scale_ref, s32[1,8]{1,0:T(1,128)} %bitcast.18, ...), custom_call_target="tpu_custom_call" | custom-call | tf_op jit(solution)/shard_map/pallas_call | solution.py:746

commit v3 on v2

--- a/solution.py
+++ b/solution.py
@@ -173,6 +173,19 @@
         )
         return carry
 
+    inner = (gy == 1) | (gy == 2)
+
+    @pl.when(inner)
+    def _():
+        def greet_far(step, carry):
+            section = lax.rem(gz + step, SECTIONS)
+            pl.semaphore_signal(
+                barrier, inc=1, device_id={"gz": section, "gy": far_gy}, device_id_type=MESH
+            )
+            return carry
+
+        lax.fori_loop(1, SECTIONS, greet_far, 0)
+
     pl.semaphore_signal(barrier, inc=1, device_id={"gy": far_gy}, device_id_type=MESH)
     lax.fori_loop(1, SECTIONS, greet, 0)
     for step in range(1, 8):
@@ -243,7 +256,13 @@
     fill(0, table_smem)
     to_vector.wait()
     holds, mine = chunk_of(gz)
-    pl.semaphore_wait(barrier, SECTIONS - 1 + 8)
+    @pl.when(inner)
+    def _():
+        pl.semaphore_wait(barrier, 2 * (SECTIONS - 1) + 8)
+
+    @pl.when(jnp.logical_not(inner))
+    def _():
+        pl.semaphore_wait(barrier, SECTIONS - 1 + 8)
 
     def scatter(step, carry):
         chunk = lax.rem(mine + step, CHUNKS)
@@ -302,9 +321,9 @@
         slots_ref[kind, place] = outgoing[kind, place]
         info_ref[kind, place] = tables[kind]
 
+    lax.fori_loop(0, CHUNKS, scatter, 0)
     table_far.start()
     to_far.start()
-    lax.fori_loop(0, CHUNKS, scatter, 0)
 
     @pl.when(core == 0)
     def _():
@@ -315,6 +334,12 @@
         own_up.start()
 
     send_slots(0)
+
+    first_row = jnp.where(gy == 1, 2, 0)
+    rim_chunk = mine - 5 * first_row
+    holds_rim = holds & inner & (rim_chunk >= 0) & (rim_chunk < 15)
+    rim_chunk = jnp.where(holds_rim, rim_chunk, 0)
+    rim_row = jnp.where(gy == 1, 0, HALO_ROWS + HEIGHT)
 
     @pl.when(holds)
     def _():
@@ -337,6 +362,22 @@
             ).start()
             return carry
 
+        def deliver_far(step, carry):
+            section = lax.rem(gz + step, SECTIONS)
+            pltpu.make_async_remote_copy(
+                src_ref=sorted_.at[section],
+                dst_ref=chunk_at(other_ref, rim_chunk, rim_row, LANES),
+                send_sem=send_sem.at[2],
+                recv_sem=recv_sem.at[2],
+                device_id={"gz": section, "gy": far_gy},
+                device_id_type=MESH,
+            ).start()
+            return carry
+
+        def send_far():
+            lax.fori_loop(0, SECTIONS, deliver_far, 0)
+
+        pl.when(holds_rim)(send_far)
         lax.fori_loop(1, SECTIONS, deliver, 0)
         chunk_at(other_ref, mine, HALO_ROWS, LANES)[...] = sorted_[gz]
 
@@ -379,15 +420,32 @@
 
     chunks = held.at[pl.ds(0, CHUNKS)]
     fewer = held.at[pl.ds(0, CHUNKS - 1)]
-    rows_up = pl.ds(HALO_ROWS, HALO_ROWS)
-    rows_down = pl.ds(HEIGHT, HALO_ROWS)
-    other_down = copy(
-        other_ref.at[rows_down, middle], other_ref.at[top, middle], 5, {"gy": jnp.minimum(gy + 1, 3)}
+    near_from = pl.ds(pl.multiple_of(HEIGHT - (HEIGHT - HALO_ROWS) * core, 16), HALO_ROWS)
+    near_to = pl.ds(pl.multiple_of((HALO_ROWS + HEIGHT) * core, 16), HALO_ROWS)
+    rest_rows = pl.ds(pl.multiple_of(HALO_ROWS * core, 16), HALO_ROWS + HEIGHT)
+    from_right, from_left = pl.ds(WIDTH, LANES), pl.ds(LANES, LANES)
+    after, before = jnp.minimum(gx + 1, 3), jnp.maximum(gx - 1, 0)
+    other_near = copy(
+        other_ref.at[near_from, middle], other_ref.at[near_to, middle], 5, {"gy": near_gy}
     )
-    other_up = copy(
-        other_ref.at[rows_up, middle], other_ref.at[bottom, middle], 6, {"gy": jnp.maximum(gy - 1, 0)}
-    )
-    other_sides = side_copies(other_ref, 7)
+    other_right = [
+        copy(other_ref.at[rest_rows, from_right], other_ref.at[rest_rows, left], 6, {"gx": after}),
+        copy(
+            other_ref.at[near_from, from_right],
+            other_ref.at[near_to, left],
+            7,
+            {"gy": near_gy, "gx": after},
+        ),
+    ]
+    other_left = [
+        copy(other_ref.at[rest_rows, from_left], other_ref.at[rest_rows, right], 8, {"gx": before}),
+        copy(
+            other_ref.at[near_from, from_left],
+            other_ref.at[near_to, right],
+            9,
+            {"gy": near_gy, "gx": before},
+        ),
+    ]
     own_sides = side_copies(own_ref, 3)
 
     def pass_rows():
@@ -399,24 +457,35 @@
         def _():
             pltpu.make_async_copy(chunks, chunks, recv_sem.at[1]).wait()
 
-        @pl.when(gy < 3)
-        def _():
-            other_down.start()
-
-        @pl.when(gy > 0)
-        def _():
-            other_up.start()
-
-    def pass_columns():
-        @pl.when(gy > 0)
-        def _():
-            other_down.wait_recv()
-
-        @pl.when(gy < 3)
-        def _():
-            other_up.wait_recv()
-
-        start_sides(other_sides)
+        @pl.when(inner)
+        def _():
+            rim = held.at[pl.ds(0, 15)]
+            pltpu.make_async_copy(rim, rim, recv_sem.at[2]).wait()
+
+        other_near.start()
+
+        @pl.when(gx < 3)
+        def _():
+            for one in other_right:
+                one.start()
+
+        @pl.when(gx > 0)
+        def _():
+            for one in other_left:
+                one.start()
+
+    def receive_rims():
+        other_near.wait_recv()
+
+        @pl.when(gx > 0)
+        def _():
+            for one in other_right:
+                one.wait_recv()
+
+        @pl.when(gx < 3)
+        def _():
+            for one in other_left:
+                one.wait_recv()
 
     def take_mirror():
         @pl.when(core == 1)
@@ -477,8 +546,7 @@
     own_spectra()
     pass_rows()
     warp()
-    pass_columns()
-    receive_sides(other_sides)
+    receive_rims()
 
     for kind in range(2):
         seven, seven_info = slots_ref.at[kind, pl.ds(0, 7)], info_ref.at[kind, pl.ds(0, 7)]
@@ -506,16 +574,24 @@
     to_far.wait_send()
     table_far.wait_send()
 
-    @pl.when(gy < 3)
-    def _():
-        other_down.wait_send()
-
-    @pl.when(gy > 0)
-    def _():
-        other_up.wait_send()
+    other_near.wait_send()
+
+    @pl.when(gx < 3)
+    def _():
+        for one in other_right:
+            one.wait_send()
+
+    @pl.when(gx > 0)
+    def _():
+        for one in other_left:
+            one.wait_send()
+
+    @pl.when(holds_rim)
+    def _():
+        every = held.at[pl.ds(0, SECTIONS)]
+        pltpu.make_async_copy(every, every, send_sem.at[2]).wait()
 
     sent_sides(own_sides)
-    sent_sides(other_sides)
     for store in stores:
         store.wait()
 
@@ -723,9 +799,9 @@
             pltpu.VMEM((4, 128, LANES), f32),
             pltpu.VMEM((HEIGHT, STRIP_COLS), f32),
             pltpu.VMEM((HEIGHT, WIDTH), f32),
-            pltpu.SemaphoreType.DMA((2,)),
-            pltpu.SemaphoreType.DMA((2,)),
-            pltpu.SemaphoreType.DMA((2, 9)),
+            pltpu.SemaphoreType.DMA((3,)),
+            pltpu.SemaphoreType.DMA((3,)),
+            pltpu.SemaphoreType.DMA((2, 10)),
             pltpu.SemaphoreType.DMA((2, 2, 2)),
             pltpu.SemaphoreType.DMA,
             pltpu.SemaphoreType.DMA((4,)),

time: 61.4 us -> 58.1 us (0.946)
  the two profiles are of different devices: /device:TPU:1 before, /device:TPU:39 now
where the time goes in v3:
time: 58.1 us; the launch traced here: 57.9 us
  Pallas kernels  57.3 us (99%)
  between operations  0.64 us (1%)
    pallas_call x1, Pallas kernels, body(): pl.pallas_call(exchange_kernel, out_shape=[jax.ShapeDtypeStruct((STRIP_RO...  48.8 us
    pallas_call x1, Pallas kernels, body(): pl.pallas_call(compute_kernel, out_shape=[jax.ShapeDtypeStruct((PATCH_COL...  8.47 us

profile of v3, /device:TPU:39, one launch (start us, length us, event | category | flops | bytes accessed | tf_op | source)
XLA Modules:
  0.0 57.9 jit_solution(15721831086344220080)
XLA Ops:
  0.6 48.8 %shard_map.158 = (bf16[176,896]{1,0:T(8,128)(2,1)}, f32[9,176,256]{2,1,0:T(8,128)}, f32[80,640]{1,0:T(8,128)}, f32[8,128]{1,0:T(8,128)}) custom-call(bf16[80,640]{1,0:T(8,128)(2,1)} %bitcast.15, s32[1,32]{1,0:T(1,128)} %bitcast.19, s32[2,8]{1,0:T(2,128)} %bitcast.16, s32[2,8]{1,0:T(2,128)} %bitcast.17, s32[1,8]{1,0:T(1,128)} %bitcast.20, ...), custom_call_target="tpu_custom_call" | custom-call | tf_op jit(solution)/shard_map/pallas_call | solution.py:769
  49.5 8.5 %shard_map.159 = (f32[8,160,160]{2,1,0:T(8,128)}, f32[80,640]{1,0:T(8,128)}) custom-call(bf16[176,896]{1,0:T(8,128)(2,1)} %get-tuple-element.8.other_ref, f32[9,176,256]{2,1,0:T(8,128)} %get-tuple-element.9.parts_hbm, f32[80,640]{1,0:T(8,128)} %get-tuple-element.10.warped_in, f32[8,128]{1,0:T(8,128)} %get-tuple-element.11.scale_ref, s32[1,8]{1,0:T(1,128)} %bitcast.18, ...), custom_call_target="tpu_custom_call" | custom-call | tf_op jit(solution)/shard_map/pallas_call | solution.py:822

commit v4 on v3

--- a/solution.py
+++ b/solution.py
@@ -264,8 +264,19 @@
     def _():
         pl.semaphore_wait(barrier, SECTIONS - 1 + 8)
 
+    line, upper = gz // 8, gz % 8 >= 4
+
+    def far_section(step):
+        to = jnp.where(upper, step // 4, 7 - step // 4)
+        return 8 * lax.rem(line + 2 + step % 4, 4) + to
+
+    def far_chunk(step):
+        before = jnp.maximum(step - 1, 0)
+        to = jnp.where(upper, before // 4, 5 - before // 4)
+        return jnp.where(step == 0, CHUNKS - 1, 6 * lax.rem(line + 2 + before % 4, 4) + to)
+
     def scatter(step, carry):
-        chunk = lax.rem(mine + step, CHUNKS)
+        chunk = far_chunk(step)
         holder = holder_of(chunk)
 
         @pl.when(holder != gz)
@@ -351,15 +362,19 @@
             sorted_[section] = held[partner_ref[0, section]]
 
         def deliver(step, carry):
-            section = lax.rem(gz + step, SECTIONS)
-            pltpu.make_async_remote_copy(
-                src_ref=sorted_.at[section],
-                dst_ref=chunk_at(other_ref, mine, HALO_ROWS, LANES),
-                send_sem=send_sem.at[1],
-                recv_sem=recv_sem.at[1],
-                device_id={"gz": section},
-                device_id_type=MESH,
-            ).start()
+            section = far_section(step)
+
+            @pl.when(section != gz)
+            def _():
+                pltpu.make_async_remote_copy(
+                    src_ref=sorted_.at[section],
+                    dst_ref=chunk_at(other_ref, mine, HALO_ROWS, LANES),
+                    send_sem=send_sem.at[1],
+                    recv_sem=recv_sem.at[1],
+                    device_id={"gz": section},
+                    device_id_type=MESH,
+                ).start()
+
             return carry
 
         def deliver_far(step, carry):
@@ -378,7 +393,7 @@
             lax.fori_loop(0, SECTIONS, deliver_far, 0)
 
         pl.when(holds_rim)(send_far)
-        lax.fori_loop(1, SECTIONS, deliver, 0)
+        lax.fori_loop(0, SECTIONS, deliver, 0)
         chunk_at(other_ref, mine, HALO_ROWS, LANES)[...] = sorted_[gz]
 
 

time: 58.1 us -> 56.9 us (0.979)
  the two profiles are of different devices: /device:TPU:39 before, /device:TPU:1 now
where the time goes in v4:
time: 56.9 us; the launch traced here: 56.8 us
  Pallas kernels  56.1 us (99%)
  between operations  0.64 us (1%)
    pallas_call x1, Pallas kernels, body(): pl.pallas_call(exchange_kernel, out_shape=[jax.ShapeDtypeStruct((STRIP_RO...  47.6 us
    pallas_call x1, Pallas kernels, body(): pl.pallas_call(compute_kernel, out_shape=[jax.ShapeDtypeStruct((PATCH_COL...  8.47 us

profile of v4, /device:TPU:1, one launch (start us, length us, event | category | flops | bytes accessed | tf_op | source)
XLA Modules:
  0.0 56.8 jit_solution(6535137280819190927)
XLA Ops:
  0.6 47.6 %shard_map.158 = (bf16[176,896]{1,0:T(8,128)(2,1)}, f32[9,176,256]{2,1,0:T(8,128)}, f32[80,640]{1,0:T(8,128)}, f32[8,128]{1,0:T(8,128)}) custom-call(bf16[80,640]{1,0:T(8,128)(2,1)} %bitcast.15, s32[1,32]{1,0:T(1,128)} %bitcast.19, s32[2,8]{1,0:T(2,128)} %bitcast.16, s32[2,8]{1,0:T(2,128)} %bitcast.17, s32[1,8]{1,0:T(1,128)} %bitcast.20, ...), custom_call_target="tpu_custom_call" | custom-call | tf_op jit(solution)/shard_map/pallas_call | solution.py:784
  48.3 8.5 %shard_map.159 = (f32[8,160,160]{2,1,0:T(8,128)}, f32[80,640]{1,0:T(8,128)}) custom-call(bf16[176,896]{1,0:T(8,128)(2,1)} %get-tuple-element.8.other_ref, f32[9,176,256]{2,1,0:T(8,128)} %get-tuple-element.9.parts_hbm, f32[80,640]{1,0:T(8,128)} %get-tuple-element.10.warped_in, f32[8,128]{1,0:T(8,128)} %get-tuple-element.11.scale_ref, s32[1,8]{1,0:T(1,128)} %bitcast.18, ...), custom_call_target="tpu_custom_call" | custom-call | tf_op jit(solution)/shard_map/pallas_call | solution.py:837

commit v5 on v4

--- a/solution.py
+++ b/solution.py
@@ -72,8 +72,8 @@
     back_rows = np.zeros((PATCH_SIZE, 2 * WAVES))
     back_rows[:, :81] = (weight[:, None] * cosine).T
     back_rows[:, WAVES : WAVES + 81] = -(weight[:, None] * sine).T
-    back_rows = halves(back_rows)
-    return (rows_both, row_sums, columns_twice, columns_low, *back_columns, *back_rows)
+    back_rows = np.concatenate(halves(back_rows), axis=0)
+    return (rows_both, row_sums, columns_twice, columns_low, *back_columns, back_rows)
 
 
 def fill_table(owner_ref, cell_ref, count_ref, flow_ref, table_ref):
@@ -703,8 +703,8 @@
 
 
 def compute_kernel(other_ref, parts_hbm, warped_in, scale_ref, mask_ref, *rest):
-    tables_hbm, (correlation_hbm, warped_hbm), rest = rest[:8], rest[8:10], rest[10:]
-    tables_vmem, rest = rest[:8], rest[8:]
+    tables_hbm, (correlation_hbm, warped_hbm), rest = rest[:7], rest[7:9], rest[9:]
+    tables_vmem, rest = rest[:7], rest[7:]
     strip, spectra, own_parts, parts, result, table_sem, part_sem, out_sem = rest
     loads = [
         pltpu.make_async_copy(src, dst, table_sem.at[index])
@@ -716,11 +716,12 @@
     own_load.start()
     stores = [pltpu.make_async_copy(warped_in, warped_hbm, out_sem.at[PATCH_COLS])]
     stores[0].start()
-    back_columns_high, back_columns_low, back_rows_high, back_rows_low = tables_vmem[4:]
-    for load in loads:
+    back_columns_high, back_columns_low, back_rows = tables_vmem[4:]
+    for load in loads[:4]:
         load.wait()
     scales = forward(other_ref, strip, spectra, parts, *tables_vmem[:4])
-    own_load.wait()
+    for load in [*loads[4:], own_load]:
+        load.wait()
 
     row = lax.broadcasted_iota(jnp.int32, (WAVES, LANES), 0)
     column = lax.broadcasted_iota(jnp.int32, (WAVES, LANES), 1)
@@ -754,16 +755,12 @@
             axis=0,
         )
         high, low = split(joined)
-        half = (
-            dot(high, back_columns_high[...])
-            + dot(low, back_columns_high[...])
-            + dot(high, back_columns_low[...])
-        )
+        both = dot(jnp.concatenate([high, low], axis=0), back_columns_high[...])
+        half = both[: 2 * WAVES] + both[2 * WAVES :] + dot(high, back_columns_low[...])
         high, low = split(half)
+        both = dot(back_rows[...], high)
         result[patch] = (
-            dot(back_rows_high[...], high)
-            + dot(back_rows_high[...], low)
-            + dot(back_rows_low[...], high)
+            both[:PATCH_SIZE] + both[PATCH_SIZE:] + dot(back_rows[:PATCH_SIZE, :], low)
         )
         stores.append(
             pltpu.make_async_copy(result.at[patch], correlation_hbm.at[patch], out_sem.at[patch])
@@ -840,7 +837,7 @@
             jax.ShapeDtypeStruct((PATCH_COLS, PATCH_SIZE, PATCH_SIZE), f32),
             jax.ShapeDtypeStruct((HEIGHT, WIDTH), f32),
         ],
-        in_specs=[VMEM, ANY, ANY, VMEM, SMEM] + [ANY] * 8,
+        in_specs=[VMEM, ANY, ANY, VMEM, SMEM] + [ANY] * 7,
         out_specs=[ANY, ANY],
         scratch_shapes=space
         + [
@@ -849,7 +846,7 @@
             pltpu.VMEM(parts_shape, f32),
             pltpu.VMEM(parts_shape, f32),
             pltpu.VMEM((PATCH_COLS, PATCH_SIZE, PATCH_SIZE), f32),
-            pltpu.SemaphoreType.DMA((8,)),
+            pltpu.SemaphoreType.DMA((7,)),
             pltpu.SemaphoreType.DMA,
             pltpu.SemaphoreType.DMA((PATCH_COLS + 1,)),
         ],

time: 56.9 us -> 56.9 us (level)
  no operation moved by 1% of the time
where the time goes in v5:
time: 56.9 us; the launch traced here: 56.7 us
  Pallas kernels  56.1 us (99%)
  between operations  0.64 us (1%)
    pallas_call x1, Pallas kernels, body(): pl.pallas_call(exchange_kernel, out_shape=[jax.ShapeDtypeStruct((STRIP_RO...  47.6 us
    pallas_call x1, Pallas kernels, body(): pl.pallas_call(compute_kernel, out_shape=[jax.ShapeDtypeStruct((PATCH_COL...  8.46 us

profile of v5, /device:TPU:1, one launch (start us, length us, event | category | flops | bytes accessed | tf_op | source)
XLA Modules:
  0.0 56.7 jit_solution(6211814332132523628)
XLA Ops:
  0.6 47.6 %shard_map.149 = (bf16[176,896]{1,0:T(8,128)(2,1)}, f32[9,176,256]{2,1,0:T(8,128)}, f32[80,640]{1,0:T(8,128)}, f32[8,128]{1,0:T(8,128)}) custom-call(bf16[80,640]{1,0:T(8,128)(2,1)} %bitcast.15, s32[1,32]{1,0:T(1,128)} %bitcast.19, s32[2,8]{1,0:T(2,128)} %bitcast.16, s32[2,8]{1,0:T(2,128)} %bitcast.17, s32[1,8]{1,0:T(1,128)} %bitcast.20, ...), custom_call_target="tpu_custom_call" | custom-call | tf_op jit(solution)/shard_map/pallas_call | solution.py:781
  48.3 8.5 %shard_map.150 = (f32[8,160,160]{2,1,0:T(8,128)}, f32[80,640]{1,0:T(8,128)}) custom-call(bf16[176,896]{1,0:T(8,128)(2,1)} %get-tuple-element.8.other_ref, f32[9,176,256]{2,1,0:T(8,128)} %get-tuple-element.9.parts_hbm, f32[80,640]{1,0:T(8,128)} %get-tuple-element.10.warped_in, f32[8,128]{1,0:T(8,128)} %get-tuple-element.11.scale_ref, s32[1,8]{1,0:T(1,128)} %bitcast.18, ...), custom_call_target="tpu_custom_call" | custom-call | tf_op jit(solution)/shard_map/pallas_call | solution.py:834
